TPU v7x, 128 devices: a whole 4x4x4 slice. The times are simulated.
128 devices in a mesh: gx: 4 (over y_lo, core), gy: 8 (over y_hi, x), gz: 4 (over z).
Axes of the slice: x: 4, y: 4 (y_hi: 2, y_lo: 2; y = y_hi * 2 + y_lo), z: 4, core: 2. Of those that a mesh axis runs over, the one named last changes fastest.
Arguments:
- species: int32 [16384], P(('gx', 'gy', 'gz')), may hold values from 0 to 7
- send_list: int32 [8, 16, 8, 4], P('gx', 'gy', 'gz'), may hold values from 0 to 127, as said below
- neighbours: int32 [16, 16384], P(None, ('gx', 'gy', 'gz')), may hold values from 0 to 383, as said below
- edge_vectors: float32 [3, 16, 16384], P(None, None, ('gx', 'gy', 'gz')), may hold values from -6 to 6, as said below
- embedding: bfloat16 [8, 128], replicated, may hold values from -6 to 6
- radial_in: float32 [2, 8, 64], replicated, may hold values from -3 to 3
- radial_mid: float32 [2, 64, 64], replicated, may hold values from -1 to 1
- radial_out: float32 [2, 64, 384], replicated, may hold values from -1.5 to 1.5
- mixing: float32 [2, 384, 128], replicated, may hold values from -0.3125 to 0.3125
- read_linear: float32 [128], replicated, may hold values from -0.5 to 0.5
- read_hidden: float32 [128, 16], replicated, may hold values from -0.5 to 0.5
- read_out: float32 [16], replicated, may hold values from -2 to 2
Outputs:
- site_energy: float32 [16384], P(('gx', 'gy', 'gz'))
- forces: float32 [3, 16384], P(None, ('gx', 'gy', 'gz'))
Inputs may be any that keep to these rules, and one draw needn't show every extreme that they name: `send_list`: each domain's 8 * 4 entries name different owned atoms. `neighbours`: A slot names an owned atom other than the atom itself (rows below 128) or a row of one of the 56 cells with some q equal to 0 or 3. Atoms whose index within their domain is below 64 name owned atoms only. `edge_vectors`: live slots are 0.75 to 4.95 long, the others 5.25 to 5.95.
All inputs are finite; a program needn't handle non-finite values.
Results may differ from a plain program's by a relative error of at most 0.0041.
Values may be sent and summed in bfloat16 or wider, within the bound.
A program may use at most 128 MiB of HBM per device.

v0:
```python
import functools
import itertools

import jax
import jax.numpy as jnp
from jax import lax
from jax.experimental import pallas as pl
from jax.experimental.pallas import tpu as pltpu
from jax.sharding import PartitionSpec as P

CUTOFF = 5.0
AXES = ("gx", "gy", "gz")
F32 = jnp.float32
BF16 = jnp.bfloat16
MESH = pl.DeviceIdType.MESH
ROOT3 = 3.0**0.5
ROOT5 = 5.0**0.5
ROOT15 = 15.0**0.5
PI = 3.141592653589793


def plan_slabs(cell_rows):
    picks = {1: (1,), -1: (0,), 0: (0, 1)}
    slabs, offset = [], 0
    for count in (1, 2, 3):
        for step in itertools.product((-1, 0, 1), repeat=3):
            if sum(s != 0 for s in step) != count:
                continue
            cells = list(itertools.product(*[picks[s] for s in step]))
            if len(cells) == 1:
                cells.append(None)
            blocks = [tuple(cells[i : i + 2]) for i in range(0, len(cells), 2)]
            slabs.append((step, offset, 8 * len(blocks), blocks))
            offset += 8 * len(blocks)
    return slabs, offset


def ghost_row(step, cell, atoms, cell_rows):
    spots = [{1: 0, -1: 3, 0: c + 1}[s] for s, c in zip(step, cell)]
    return atoms + (16 * spots[0] + 4 * spots[1] + spots[2]) * cell_rows


def split_rows(x):
    high = x.astype(BF16).astype(F32)
    return jnp.concatenate([high, x - high, high], axis=0).astype(BF16)


def weight_rows(w):
    high = w.astype(BF16).astype(F32)
    return jnp.concatenate([high, high, w - high], axis=0)


def dot(a, b):
    return lax.dot_general(a, b, (((1,), (0,)), ((), ())), preferred_element_type=F32)


def dot_nt(a, b):
    return lax.dot_general(a, b, (((1,), (1,)), ((), ())), preferred_element_type=F32)


def loop(count, body):
    def step(i, carry):
        body(i)
        return carry

    lax.fori_loop(0, count, step, 0)


def kernel(
    sizes,
    species,
    send_list,
    neighbours,
    vectors,
    embedding,
    radial_in,
    radial_mid,
    radial_out,
    mixing,
    read_linear,
    read_hidden,
    read_out,
    site_out,
    force_out,
    basis,
    cut,
    harm,
    rad,
    drad,
    oh_own,
    oh_ghost,
    feat,
    amp,
    inv,
    cot_feat,
    acc_ref,
    grad_cat,
    sel,
    w_in,
    w_mid,
    w_out,
    mix_t,
    mix_c,
    first_ref,
    send_buf,
    recv_buf,
    send_sem,
    recv_sem,
):
    atoms = species.shape[1]
    half = atoms // 2
    channels = embedding.shape[1]
    pairs = neighbours.shape[0] // 2
    cell_rows = send_list.shape[3]
    hidden = radial_mid.shape[1]
    slabs, ghosts = plan_slabs(cell_rows)
    me = [lax.axis_index(axis) for axis in AXES]

    def at(step):
        return tuple(
            m if s == 0 else lax.rem(m + (s + n), n) for m, s, n in zip(me, step, sizes)
        )

    barrier = pltpu.get_barrier_semaphore()
    for step, _, _, _ in slabs:
        pl.semaphore_signal(barrier, inc=1, device_id=at(step), device_id_type=MESH)

    def send(phase, back):
        for step, offset, rows, _ in slabs:
            goal = tuple(-s for s in step) if back else step
            pltpu.make_async_remote_copy(
                src_ref=send_buf.at[phase, pl.ds(offset, rows)],
                dst_ref=recv_buf.at[phase, pl.ds(offset, rows)],
                send_sem=send_sem.at[phase],
                recv_sem=recv_sem.at[phase],
                device_id=at(goal),
                device_id_type=MESH,
            ).start()

    def wait_in(phase):
        whole = recv_buf.at[phase]
        pltpu.make_async_copy(whole, whole, recv_sem.at[phase]).wait()

    def wait_out(phase):
        whole = send_buf.at[phase]
        pltpu.make_async_copy(whole, whole, send_sem.at[phase]).wait()

    lane = lax.broadcasted_iota(jnp.int32, (8, atoms), 1)
    sub = lax.broadcasted_iota(jnp.int32, (8, atoms), 0)
    low8 = lane < half

    def low_of(x):
        return lax.broadcasted_iota(jnp.int32, x.shape, 1) < half

    def turn(x):
        return pltpu.roll(x, half, 1)

    def dup(x, group):
        if group == 0:
            return jnp.where(low_of(x), x, turn(x))
        return jnp.where(low_of(x), turn(x), x)

    def paired(x):
        top, bottom = x[:pairs], x[pairs:]
        return (
            jnp.where(low8, top, turn(bottom)),
            jnp.where(low8, turn(top), bottom),
        )

    cell_ids = {}
    spot = sub % cell_rows
    for cell in itertools.product((0, 1), repeat=3):
        value = jnp.full((8, atoms), send_list[cell + (0,)], jnp.int32)
        for k in range(1, cell_rows):
            value = jnp.where(spot == k, send_list[cell + (k,)], value)
        cell_ids[cell] = value
    cell_ids[None] = jnp.full((8, atoms), -1, jnp.int32)
    row_ids = []
    chosen = []
    for step, offset, rows, blocks in slabs:
        for cell_a, cell_b in blocks:
            ids = jnp.where(sub < cell_rows, cell_ids[cell_a], cell_ids[cell_b])
            chosen.append(jnp.where(ids == lane, 1.0, 0.0))
            base_a = ghost_row(step, cell_a, atoms, cell_rows) + sub
            if cell_b is None:
                base_b = jnp.full((8, atoms), -1, jnp.int32)
            else:
                base_b = ghost_row(step, cell_b, atoms, cell_rows) + sub - cell_rows
            row_ids.append(jnp.where(sub < cell_rows, base_a, base_b))
    sel[...] = jnp.concatenate(chosen, axis=0).astype(BF16)

    kinds = jnp.where(sub == jnp.broadcast_to(species[...], (8, atoms)), 1.0, 0.0).astype(BF16)
    emb_t = embedding[...].astype(F32).T.astype(BF16)
    start_t = dot(emb_t, kinds)
    send_buf[0] = dot_nt(sel[...], start_t.astype(BF16))

    for t in range(2):
        pad = jnp.zeros((8, hidden), F32)
        w_in[t * hidden : (t + 1) * hidden] = (
            jnp.concatenate([weight_rows(radial_in[t]), pad], axis=0).T.astype(BF16)
        )
        w_mid[t] = weight_rows(radial_mid[t]).T.astype(BF16)
        w_out[t] = weight_rows(radial_out[t]).T.astype(BF16)

    vec = [paired(vectors[k]) for k in range(3)]
    nbr = paired(neighbours[...])
    geo = []
    for g in range(2):
        x, y, z = vec[0][g], vec[1][g], vec[2][g]
        length = jnp.sqrt(x * x + y * y + z * z)
        over = 1.0 / length
        nx, ny, nz = x * over, y * over, z * over
        geo.append((nx, ny, nz, over))
        u = length * (1.0 / CUTOFF)
        u2 = u * u
        u4 = u2 * u2
        u5 = u4 * u
        inside = u < 1.0
        env = 1.0 - 21.0 * u5 + 35.0 * u5 * u - 15.0 * u5 * u2
        denv = (-105.0 / CUTOFF) * u4 * (1.0 - u) * (1.0 - u)
        cut[g, 0] = jnp.where(inside, 0.25 * env, 0.0)
        cut[g, 1] = jnp.where(inside, 0.25 * denv, 0.0)
        theta = PI * u
        sin1, cos1 = jnp.sin(theta), jnp.cos(theta)
        twice = 2.0 * cos1
        s_old, s_now = jnp.zeros_like(sin1), sin1
        c_old, c_now = jnp.ones_like(cos1), cos1
        amp0 = (2.0 / CUTOFF) ** 0.5
        for k in range(1, 9):
            base = amp0 * s_now * over
            slope = (amp0 * k * PI / CUTOFF * c_now - base) * over
            basis[g, 0, (k - 1) * 8 : k * 8] = base
            basis[g, 1, (k - 1) * 8 : k * 8] = slope
            s_old, s_now = s_now, twice * s_now - s_old
            c_old, c_now = c_now, twice * c_now - c_old
        ylm = (
            ROOT3 * nx,
            ROOT3 * ny,
            ROOT3 * nz,
            ROOT15 * nx * ny,
            ROOT15 * ny * nz,
            0.5 * ROOT5 * (3.0 * nz * nz - 1.0),
            ROOT15 * nx * nz,
            0.5 * ROOT15 * (nx * nx - ny * ny),
        )
        for m in range(8):
            for p in range(pairs):
                harm[g * pairs + p, m * 8 : (m + 1) * 8] = jnp.broadcast_to(
                    ylm[m][p : p + 1], (8, atoms)
                )

    own_rows = jnp.concatenate([sub + 8 * b for b in range(atoms // 8)], axis=0)
    all_rows = jnp.concatenate([own_rows] + row_ids, axis=0)
    for p in range(pairs):
        lanes = slice(p * atoms, (p + 1) * atoms)
        oh_own[:, lanes] = jnp.where(own_rows == nbr[0][p : p + 1], 1.0, 0.0).astype(BF16)
        oh_ghost[:, lanes] = jnp.where(all_rows == nbr[1][p : p + 1], 1.0, 0.0).astype(BF16)

    pl.semaphore_wait(barrier, len(slabs))
    send(0, False)

    def silu_pair(x, dx):
        gate = 0.5 + 0.5 * jnp.tanh(0.5 * x)
        value = x * gate
        return value, gate * (1.0 + x - value) * dx

    def radial(g):
        def chunk(j):
            def wide(ref, kind):
                return jnp.concatenate(
                    [ref[g, kind, pl.ds(2 * j + i, 8, stride=8), :] for i in range(2)], axis=1
                )

            def row(kind):
                return jnp.concatenate(
                    [cut[g, kind, pl.ds(2 * j + i, 1), :] for i in range(2)], axis=1
                )

            env, denv = row(0), row(1)
            pad = jnp.zeros((8, 2 * atoms), BF16)

            def first_dot(x):
                high = x.astype(BF16).astype(F32)
                full = jnp.concatenate([high, x - high, high, jnp.zeros_like(x)], axis=0)
                return dot(w_in[...], full.astype(BF16))

            one, done = silu_pair(first_dot(wide(basis, 0)), first_dot(wide(basis, 1)))
            for t in range(2):
                rows = slice(t * hidden, (t + 1) * hidden)
                two, dtwo = silu_pair(
                    dot(w_mid[t], split_rows(one[rows])), dot(w_mid[t], split_rows(done[rows]))
                )
                value = dot(w_out[t], split_rows(env * two))
                slope = dot(w_out[t], split_rows(denv * two + env * dtwo))
                for i in range(2):
                    lanes = slice(i * atoms, (i + 1) * atoms)
                    rad[(t * 2 + g) * pairs + 2 * j + i] = value[:, lanes]
                    drad[(t * 2 + g) * pairs + 2 * j + i] = slope[:, lanes]

        loop(pairs // 2, chunk)

    radial(0)
    radial(1)
    for t in range(2):
        mix_t[t] = weight_rows(mixing[t]).T.astype(BF16)
        high = mixing[t].astype(BF16).astype(F32)
        mix_c[t] = jnp.concatenate([high, high, mixing[t] - high], axis=1).astype(BF16)
    rl_col = jnp.broadcast_to(read_linear[...], (channels, channels)).T
    rh = read_hidden[...]
    rh_t = weight_rows(rh).T.astype(BF16)
    rh_high = rh.astype(BF16).astype(F32)
    rh_c = jnp.concatenate([rh_high, rh_high, rh - rh_high], axis=1).astype(BF16)
    ro_col = jnp.broadcast_to(read_out[...], (channels, read_out.shape[1])).T

    def gather(t, g, own_t, ghost_t):
        base = (t * 2 + g) * pairs

        def chunk(j):
            lanes = pl.ds(pl.multiple_of(j * 2 * atoms, 2 * atoms), 2 * atoms)
            if g == 0:
                out = dot(own_t, oh_own[:, lanes])
            else:
                out = dot(own_t, oh_ghost[:atoms, lanes]) + dot(ghost_t, oh_ghost[atoms:, lanes])
            feat[base + 2 * j] = out[:, :atoms]
            feat[base + 2 * j + 1] = out[:, atoms:]

        loop(pairs // 2, chunk)

    def twin(y):
        return jnp.concatenate([y, y], axis=0)

    def forward(t, g):
        which = t * 2 + g
        base = which * pairs

        def block(b):
            row = pl.multiple_of(b * 16, 16)

            def rows(l):
                return pl.ds(pl.multiple_of(row + l * channels, 16), 16)

            total = [jnp.zeros((16, atoms), F32) for _ in range(9)]
            for p in range(pairs):
                v = feat[base + p, rows(0)]
                parts = [rad[base + p, rows(l)] * v for l in range(3)]
                total[0] = total[0] + parts[0]
                for m in range(8):
                    y = twin(harm[g * pairs + p, m * 8 : (m + 1) * 8])
                    total[1 + m] = total[1 + m] + y * parts[1 if m < 3 else 2]
            total = [a + turn(a) for a in total]
            for m in range(1, 9):
                amp[which, m, rows(0)] = total[m]
            inv[rows(0)] = total[0]
            inv[rows(1)] = sum(a * a for a in total[1:4])
            inv[rows(2)] = sum(a * a for a in total[4:9])

        loop(channels // 16, block)

    def back_amp(t, g, dinv):
        which = t * 2 + g
        inv[...] = dinv

        def block(b):
            row = pl.multiple_of(b * 16, 16)

            def rows(l):
                return pl.ds(pl.multiple_of(row + l * channels, 16), 16)

            amp[which, 0, rows(0)] = inv[rows(0)]
            d1 = 2.0 * inv[rows(1)]
            d2 = 2.0 * inv[rows(2)]
            for m in range(1, 9):
                amp[which, m, rows(0)] = amp[which, m, rows(0)] * (d1 if m < 4 else d2)

        loop(channels // 16, block)

    def backward(t, g):
        which = t * 2 + g
        base = which * pairs

        def slot(p):
            ys = [twin(harm[g * pairs + p, m * 8 : (m + 1) * 8]) for m in range(8)]
            total = [jnp.zeros((16, atoms), F32) for _ in range(9)]
            lanes = pl.ds(pl.multiple_of(p * atoms, atoms), atoms)
            for c in range(0, channels, 16):
                rows = slice(c, c + 16)
                v = feat[base + p, rows]
                r = [rad[base + p, l * channels + c : l * channels + c + 16] for l in range(3)]
                q = [drad[base + p, l * channels + c : l * channels + c + 16] for l in range(3)]
                d = [amp[which, m, rows] for m in range(9)]
                t1 = ys[0] * d[1] + ys[1] * d[2] + ys[2] * d[3]
                t2 = ys[3] * d[4] + ys[4] * d[5] + ys[5] * d[6] + ys[6] * d[7] + ys[7] * d[8]
                if t == 1:
                    cot_feat[g, rows, lanes] = (r[0] * d[0] + r[1] * t1 + r[2] * t2).astype(BF16)
                total[0] = total[0] + v * (q[0] * d[0] + q[1] * t1 + q[2] * t2)
                p1, p2 = v * r[1], v * r[2]
                for m in range(1, 9):
                    total[m] = total[m] + (p1 if m < 4 else p2) * d[m]
            for m in range(9):
                part = total[m][:8] + total[m][8:]
                spots = pl.ds(pl.multiple_of(p * 8, 8), 8)
                if t == 1:
                    acc_ref[g, m, spots] = part
                else:
                    acc_ref[g, m, spots] = acc_ref[g, m, spots] + part

        loop(pairs, slot)

    start_b = start_t.astype(BF16)
    gather(0, 0, start_b, None)
    forward(0, 0)
    inv_own = inv[...]
    wait_in(0)
    gather(0, 1, start_b, recv_buf[0].T.astype(BF16))
    forward(0, 1)
    inv_both = jnp.where(low_of(inv_own), inv_own, inv[...])
    first_b = (start_t + dot(mix_t[0], split_rows(inv_both))).astype(BF16)
    send_buf[1] = dot_nt(sel[...], first_b)
    send(1, False)
    first_ref[...] = first_b.astype(F32)

    def energy(g):
        own = dup(first_ref[...], g)
        second = own + dot(mix_t[1], split_rows(inv[...]))
        act = dot(rh_t, split_rows(second))
        gate = 0.5 + 0.5 * jnp.tanh(0.5 * act)
        value = act * gate
        site = jnp.sum(rl_col * own, axis=0, keepdims=True) + jnp.sum(
            ro_col * value, axis=0, keepdims=True
        )
        dact = ro_col * gate * (1.0 + act - value)
        dsecond = dot(rh_c, split_rows(dact))
        return site, rl_col + dsecond, dot(mix_c[1], split_rows(dsecond))

    gather(1, 0, first_b, None)
    forward(1, 0)
    site_own, cot_own, dinv = energy(0)
    back_amp(1, 0, dinv)
    backward(1, 0)
    wait_in(1)
    gather(1, 1, first_ref[...].astype(BF16), recv_buf[1].T.astype(BF16))
    forward(1, 1)
    site_ghost, cot_ghost, dinv = energy(1)
    back_amp(1, 1, dinv)
    backward(1, 1)
    send_buf[2] = dot_nt(oh_ghost[atoms:], cot_feat[1])
    send(2, True)
    site_out[...] = jnp.where(low_of(site_own), site_own, site_ghost)
    cot = jnp.where(low_of(cot_own), cot_own, cot_ghost)
    cot = cot + dot_nt(cot_feat[0], oh_own[...]) + dot_nt(cot_feat[1], oh_ghost[:atoms])
    send_buf[3] = jnp.zeros((ghosts, atoms), F32)
    wait_in(2)
    back = recv_buf[2].T
    high = back.astype(BF16).astype(F32)
    parts = dot(jnp.concatenate([high, back - high], axis=0).astype(BF16), sel[...])
    cot = cot + parts[:channels] + parts[channels:]

    for g in range(2):
        back_amp(0, g, dot(mix_c[0], split_rows(dup(cot, g))))
        backward(0, g)

    sums = []
    for g in range(2):
        d = []
        for m in range(9):
            d.append(sum(acc_ref[g, m, pl.ds(j, pairs, stride=8), :] for j in range(8)))
        nx, ny, nz, over = geo[g]
        gx = ROOT3 * d[1] + ROOT15 * (ny * d[4] + nz * d[7] + nx * d[8])
        gy = ROOT3 * d[2] + ROOT15 * (nx * d[4] + nz * d[5] - ny * d[8])
        gz = ROOT3 * d[3] + ROOT15 * (ny * d[5] + nx * d[7]) + (3.0 * ROOT5) * nz * d[6]
        along = d[0] - (nx * gx + ny * gy + nz * gz) * over
        grad = [n * along + c * over for n, c in ((nx, gx), (ny, gy), (nz, gz))]
        folded = []
        for k in range(3):
            one = jnp.sum(grad[k], axis=0, keepdims=True)
            folded.append(one + turn(one))
            basis[g, 0, k * 8 : (k + 1) * 8] = -grad[k]
        sums.append(folded)
        basis[g, 0, 24:64] = jnp.zeros((40, atoms), F32)
        for p in range(pairs):
            row = basis[g, 0, pl.ds(p, 8, stride=8), :]
            high = row.astype(BF16).astype(F32)
            grad_cat[g, :, p * atoms : (p + 1) * atoms] = jnp.concatenate(
                [high, row - high], axis=0
            ).astype(BF16)
    send_buf[3, :, 0:16] = dot_nt(oh_ghost[atoms:], grad_cat[1])
    send(3, True)
    local = dot_nt(grad_cat[0], oh_own[...]) + dot_nt(grad_cat[1], oh_ghost[:atoms])
    local = local[:8] + local[8:]
    mine = jnp.concatenate(
        [jnp.where(low_of(sums[0][k]), sums[0][k], sums[1][k]) for k in range(3)], axis=0
    )
    local = local[:3] + mine
    wait_in(3)
    back = recv_buf[3].T
    back = back[:8] + back[8:16]
    high = back.astype(BF16).astype(F32)
    mid = (back - high).astype(BF16).astype(F32)
    parts = dot(jnp.concatenate([high, mid, back - high - mid], axis=0).astype(BF16), sel[...])
    force_out[...] = local + (parts[:8] + parts[8:16] + parts[16:24])[:3]
    for phase in range(4):
        wait_out(phase)


def solution(mesh):
    sizes = tuple(mesh.shape[axis] for axis in AXES)

    def body(
        species,
        send_list,
        neighbours,
        edge_vectors,
        embedding,
        radial_in,
        radial_mid,
        radial_out,
        mixing,
        read_linear,
        read_hidden,
        read_out,
    ):
        atoms = species.shape[0]
        channels = embedding.shape[1]
        slots = neighbours.shape[0]
        pairs = slots // 2
        hidden = radial_mid.shape[1]
        ghosts = plan_slabs(send_list.shape[3])[1]
        vmem = pl.BlockSpec(memory_space=pltpu.VMEM)
        smem = pl.BlockSpec(memory_space=pltpu.SMEM)
        site, forces = pl.pallas_call(
            functools.partial(kernel, sizes),
            out_shape=(
                jax.ShapeDtypeStruct((1, atoms), F32),
                jax.ShapeDtypeStruct((3, atoms), F32),
            ),
            in_specs=[vmem, smem] + [vmem] * 10,
            out_specs=(vmem, vmem),
            scratch_shapes=[
                pltpu.VMEM((2, 2, 8 * pairs, atoms), F32),
                pltpu.VMEM((2, 2, pairs, atoms), F32),
                pltpu.VMEM((2 * pairs, 64, atoms), F32),
                pltpu.VMEM((4 * pairs, 3 * channels, atoms), F32),
                pltpu.VMEM((4 * pairs, 3 * channels, atoms), F32),
                pltpu.VMEM((atoms, pairs * atoms), BF16),
                pltpu.VMEM((atoms + ghosts, pairs * atoms), BF16),
                pltpu.VMEM((4 * pairs, channels, atoms), F32),
                pltpu.VMEM((4, 9, channels, atoms), F32),
                pltpu.VMEM((3 * channels, atoms), F32),
                pltpu.VMEM((2, channels, pairs * atoms), BF16),
                pltpu.VMEM((2, 9, 8 * pairs, atoms), F32),
                pltpu.VMEM((2, 16, pairs * atoms), BF16),
                pltpu.VMEM((ghosts, atoms), BF16),
                pltpu.VMEM((2 * hidden, 32), BF16),
                pltpu.VMEM((2, hidden, 3 * hidden), BF16),
                pltpu.VMEM((2, 3 * channels, 3 * hidden), BF16),
                pltpu.VMEM((2, channels, 9 * channels), BF16),
                pltpu.VMEM((2, 3 * channels, 3 * channels), BF16),
                pltpu.VMEM((channels, atoms), F32),
                pltpu.VMEM((4, ghosts, channels), F32),
                pltpu.VMEM((4, ghosts, channels), F32),
                pltpu.SemaphoreType.DMA((4,)),
                pltpu.SemaphoreType.DMA((4,)),
            ],
            compiler_params=pltpu.CompilerParams(
                collective_id=0, has_side_effects=True, vmem_limit_bytes=56 * 1024 * 1024
            ),
        )(
            species.reshape(1, atoms),
            send_list,
            neighbours,
            edge_vectors,
            embedding,
            radial_in,
            radial_mid,
            radial_out,
            mixing,
            read_linear.reshape(1, channels),
            read_hidden,
            read_out.reshape(1, read_out.shape[0]),
        )
        return site.reshape(atoms), forces

    in_specs = (
        P(AXES),
        P("gx", "gy", "gz", None),
        P(None, AXES),
        P(None, None, AXES),
        P(),
        P(),
        P(),
        P(),
        P(),
        P(),
        P(),
        P(),
    )
    out_specs = (P(AXES), P(None, AXES))
    return jax.shard_map(body, mesh=mesh, in_specs=in_specs, out_specs=out_specs, check_vma=False)
```

profile of v0, /device:TPU:1, one launch (start us, length us, event | category | flops | bytes accessed | tf_op | source)
XLA Modules:
  0.0 48.9 jit_solution(11779663090700776109)
XLA Ops:
  0.6 1.4 %copy.14.read_hidden = f32[128,16]{1,0:T(8,128)} copy(f32[128,16]{0,1:T(8,128)} %param.22) | data formatting | bytes 16384 | tf_op args[10]
  2.0 45.2 %shard_map.131 = (f32[1,128]{1,0:T(1,128)}, f32[3,128]{1,0:T(4,128)}) custom-call(s32[1,128]{1,0:T(1,128)} %bitcast.4, s32[2,2,2,4]{3,2,1,0:T(2,128)} %send_list.1, s32[16,128]{1,0:T(8,128)} %neighbours.1, f32[3,16,128]{2,1,0:T(8,128)} %vectors.1, bf16[8,128]{1,0:T(8,128)(2,1)} %embedding.1, f32[2,8,64]{2,1,0:T(8,128)} %radial_in.1, ...), custom_call_target="tpu_custom_call" | custom-call | tf_op jit(solution)/shard_map/pallas_call | solution.py:530
  47.3 0.0 copy-start.1
  47.3 0.0 copy-start
  47.3 0.6 %copy-done.1 = f32[1,128]{1,0:T(1,128)S(1)} copy-done((f32[1,128]{1,0:T(1,128)S(1)}, f32[1,128]{1,0:T(1,128)}, u32[]{:S(2)}) %copy-start.1) | copy-done | bytes 536
  47.9 0.5 %copy.17 = f32[128]{0:T(128)} copy(f32[128]{0:T(128)S(1)} %bitcast.7) | data formatting | bytes 1024
  48.4 0.0 copy-done
  48.4 0.6 %copy.18 = f32[3,128]{1,0:T(4,128)} copy(f32[3,128]{1,0:T(4,128)S(1)} %copy-done) | data formatting | bytes 3072
Async XLA Ops:
  47.3 0.6 %copy-start.1 = (f32[1,128]{1,0:T(1,128)S(1)}, f32[1,128]{1,0:T(1,128)}, u32[]{:S(2)}) copy-start(f32[1,128]{1,0:T(1,128)} %get-tuple-element.4) | copy-start | bytes 1540
  47.3 1.1 %copy-start = (f32[3,128]{1,0:T(4,128)S(1)}, f32[3,128]{1,0:T(4,128)}, u32[]{:S(2)}) copy-start(f32[3,128]{1,0:T(4,128)} %get-tuple-element.9) | copy-start | bytes 4612
where the time goes:
time: 49.1 us; the launch traced here: 48.9 us
  Pallas kernels  45.2 us (92%)
  local copies, waits for them, and re-layouts  3.08 us (6%)
  between operations  0.66 us (1%)
    pallas_call x1, Pallas kernels, body(): pl.pallas_call(functools.partial(kernel, sizes), out_shape=(jax.ShapeDtyp...  45.2 us
    unnamed x7, local copies, waits for them, and re-layouts  3.08 us

commit v1 on v0

--- a/solution.py
+++ b/solution.py
@@ -58,12 +58,13 @@
     return lax.dot_general(a, b, (((1,), (1,)), ((), ())), preferred_element_type=F32)
 
 
+def mult(x, n):
+    return x if isinstance(x, int) else pl.multiple_of(x, n)
+
+
 def loop(count, body):
-    def step(i, carry):
+    for i in range(count):
         body(i)
-        return carry
-
-    lax.fori_loop(0, count, step, 0)
 
 
 def kernel(
@@ -307,16 +308,16 @@
         mix_c[t] = jnp.concatenate([high, high, mixing[t] - high], axis=1).astype(BF16)
     rl_col = jnp.broadcast_to(read_linear[...], (channels, channels)).T
     rh = read_hidden[...]
-    rh_t = weight_rows(rh).T.astype(BF16)
     rh_high = rh.astype(BF16).astype(F32)
-    rh_c = jnp.concatenate([rh_high, rh_high, rh - rh_high], axis=1).astype(BF16)
+    rh_t = jnp.concatenate([rh_high, rh_high, rh - rh_high], axis=1).astype(BF16)
+    rh_c = weight_rows(rh).T.astype(BF16)
     ro_col = jnp.broadcast_to(read_out[...], (channels, read_out.shape[1])).T
 
     def gather(t, g, own_t, ghost_t):
         base = (t * 2 + g) * pairs
 
         def chunk(j):
-            lanes = pl.ds(pl.multiple_of(j * 2 * atoms, 2 * atoms), 2 * atoms)
+            lanes = pl.ds(mult(j * 2 * atoms, 2 * atoms), 2 * atoms)
             if g == 0:
                 out = dot(own_t, oh_own[:, lanes])
             else:
@@ -334,10 +335,10 @@
         base = which * pairs
 
         def block(b):
-            row = pl.multiple_of(b * 16, 16)
+            row = mult(b * 16, 16)
 
             def rows(l):
-                return pl.ds(pl.multiple_of(row + l * channels, 16), 16)
+                return pl.ds(mult(row + l * channels, 16), 16)
 
             total = [jnp.zeros((16, atoms), F32) for _ in range(9)]
             for p in range(pairs):
@@ -361,10 +362,10 @@
         inv[...] = dinv
 
         def block(b):
-            row = pl.multiple_of(b * 16, 16)
+            row = mult(b * 16, 16)
 
             def rows(l):
-                return pl.ds(pl.multiple_of(row + l * channels, 16), 16)
+                return pl.ds(mult(row + l * channels, 16), 16)
 
             amp[which, 0, rows(0)] = inv[rows(0)]
             d1 = 2.0 * inv[rows(1)]
@@ -381,7 +382,7 @@
         def slot(p):
             ys = [twin(harm[g * pairs + p, m * 8 : (m + 1) * 8]) for m in range(8)]
             total = [jnp.zeros((16, atoms), F32) for _ in range(9)]
-            lanes = pl.ds(pl.multiple_of(p * atoms, atoms), atoms)
+            lanes = pl.ds(mult(p * atoms, atoms), atoms)
             for c in range(0, channels, 16):
                 rows = slice(c, c + 16)
                 v = feat[base + p, rows]
@@ -398,7 +399,7 @@
                     total[m] = total[m] + (p1 if m < 4 else p2) * d[m]
             for m in range(9):
                 part = total[m][:8] + total[m][8:]
-                spots = pl.ds(pl.multiple_of(p * 8, 8), 8)
+                spots = pl.ds(mult(p * 8, 8), 8)
                 if t == 1:
                     acc_ref[g, m, spots] = part
                 else:
@@ -575,7 +576,7 @@
             radial_out,
             mixing,
             read_linear.reshape(1, channels),
-            read_hidden,
+            read_hidden.T,
             read_out.reshape(1, read_out.shape[0]),
         )
         return site.reshape(atoms), forces

time: 49.1 us -> 43.2 us (0.88)
  Pallas kernels: 45.2 us -> 40.7 us
  local copies, waits for them, and re-layouts: 3.08 us -> 1.71 us
    pallas_call x1, Pallas kernels: 45.2 us -> 40.7 us  [body(): pl.pallas_call(functools.partial(kernel, sizes), out_shape=(jax.ShapeDtyp...]
    unnamed x7 -> x6, local copies, waits for them, and re-layouts: 3.08 us -> 1.71 us
where the time goes in v1:
time: 43.2 us; the launch traced here: 43.1 us
  Pallas kernels  40.7 us (94%)
  local copies, waits for them, and re-layouts  1.71 us (4%)
  between operations  0.66 us (2%)
    pallas_call x1, Pallas kernels, body(): pl.pallas_call(functools.partial(kernel, sizes), out_shape=(jax.ShapeDtyp...  40.7 us
    unnamed x6, local copies, waits for them, and re-layouts  1.71 us

profile of v1, /device:TPU:1, one launch (start us, length us, event | category | flops | bytes accessed | tf_op | source)
XLA Modules:
  0.0 43.1 jit_solution(7788010214294176347)
XLA Ops:
  0.6 40.7 %shard_map.131 = (f32[1,128]{1,0:T(1,128)}, f32[3,128]{1,0:T(4,128)}) custom-call(s32[1,128]{1,0:T(1,128)} %bitcast.6, s32[2,2,2,4]{3,2,1,0:T(2,128)} %send_list.1, s32[16,128]{1,0:T(8,128)} %neighbours.1, f32[3,16,128]{2,1,0:T(8,128)} %vectors.1, bf16[8,128]{1,0:T(8,128)(2,1)} %embedding.1, f32[2,8,64]{2,1,0:T(8,128)} %radial_in.1, ...), custom_call_target="tpu_custom_call" | custom-call | tf_op jit(solution)/shard_map/pallas_call | solution.py:531
  41.4 0.0 copy-start.1
  41.4 0.0 copy-start
  41.4 0.6 %copy-done.1 = f32[1,128]{1,0:T(1,128)S(1)} copy-done((f32[1,128]{1,0:T(1,128)S(1)}, f32[1,128]{1,0:T(1,128)}, u32[]{:S(2)}) %copy-start.1) | copy-done | bytes 536
  42.0 0.5 %copy.16 = f32[128]{0:T(128)} copy(f32[128]{0:T(128)S(1)} %bitcast.9) | data formatting | bytes 1024
  42.5 0.0 copy-done
  42.5 0.6 %copy.17 = f32[3,128]{1,0:T(4,128)} copy(f32[3,128]{1,0:T(4,128)S(1)} %copy-done) | data formatting | bytes 3072
Async XLA Ops:
  41.4 0.6 %copy-start.1 = (f32[1,128]{1,0:T(1,128)S(1)}, f32[1,128]{1,0:T(1,128)}, u32[]{:S(2)}) copy-start(f32[1,128]{1,0:T(1,128)} %get-tuple-element.4) | copy-start | bytes 1540
  41.4 1.1 %copy-start = (f32[3,128]{1,0:T(4,128)S(1)}, f32[3,128]{1,0:T(4,128)}, u32[]{:S(2)}) copy-start(f32[3,128]{1,0:T(4,128)} %get-tuple-element.9) | copy-start | bytes 4612

commit v2 on v1

v2 whole, which is shorter than its diff:
```python
import functools
import itertools

import jax
import jax.numpy as jnp
from jax import lax
from jax.experimental import pallas as pl
from jax.experimental.pallas import tpu as pltpu
from jax.sharding import PartitionSpec as P

CUTOFF = 5.0
AXES = ("gx", "gy", "gz")
F32 = jnp.float32
BF16 = jnp.bfloat16
MESH = pl.DeviceIdType.MESH
ROOT3 = 3.0**0.5
ROOT5 = 5.0**0.5
ROOT15 = 15.0**0.5
PI = 3.141592653589793
LOAD_ORDER = (1, 0, 4, 2, 3, 5, 6, 7, 9, 8, 10, 11)


def plan_slabs(cell_rows):
    picks = {1: (1,), -1: (0,), 0: (0, 1)}
    slabs, offset = [], 0
    for count in (1, 2, 3):
        for step in itertools.product((-1, 0, 1), repeat=3):
            if sum(s != 0 for s in step) != count:
                continue
            cells = list(itertools.product(*[picks[s] for s in step]))
            if len(cells) == 1:
                cells.append(None)
            blocks = [tuple(cells[i : i + 2]) for i in range(0, len(cells), 2)]
            slabs.append((step, offset, 8 * len(blocks), blocks))
            offset += 8 * len(blocks)
    return slabs, offset


def ghost_row(step, cell, atoms, cell_rows):
    spots = [{1: 0, -1: 3, 0: c + 1}[s] for s, c in zip(step, cell)]
    return atoms + (16 * spots[0] + 4 * spots[1] + spots[2]) * cell_rows


def split_rows(x):
    high = x.astype(BF16).astype(F32)
    return jnp.concatenate([high, x - high, high], axis=0).astype(BF16)


def weight_rows(w):
    high = w.astype(BF16).astype(F32)
    return jnp.concatenate([high, high, w - high], axis=0)


def dot(a, b):
    return lax.dot_general(a, b, (((1,), (0,)), ((), ())), preferred_element_type=F32)


def dot_nt(a, b):
    return lax.dot_general(a, b, (((1,), (1,)), ((), ())), preferred_element_type=F32)


def mult(x, n):
    return x if isinstance(x, int) else pl.multiple_of(x, n)


def loop(count, body):
    for i in range(count):
        body(i)


def kernel(
    sizes,
    operands,
    site_out,
    force_out,
    basis,
    cut,
    harm,
    rad,
    drad,
    oh_own,
    oh_ghost,
    oh_edge,
    feat,
    amp,
    cot_feat,
    acc_ref,
    grad_cat,
    sel,
    sel_b,
    rep,
    w_in,
    w_mid,
    w_out,
    mix_t,
    mix_c,
    first_ref,
    send_buf,
    recv_buf,
    send_sem,
    recv_sem,
    held,
    held_sem,
):
    (
        species,
        send_list,
        neighbours,
        vectors,
        embedding,
        radial_in,
        radial_mid,
        radial_out,
        mixing,
        read_linear,
        read_hidden,
        read_out,
    ) = held
    atoms = species.shape[1]
    half = atoms // 2
    channels = embedding.shape[1]
    pairs = neighbours.shape[0] // 2
    cell_rows = send_list.shape[3]
    hidden = radial_mid.shape[1]
    slabs, ghosts = plan_slabs(cell_rows)
    me = [lax.axis_index(axis) for axis in AXES]

    def at(step):
        return tuple(
            m if s == 0 else lax.rem(m + (s + n), n) for m, s, n in zip(me, step, sizes)
        )

    barrier = pltpu.get_barrier_semaphore()
    for step, _, _, _ in slabs:
        pl.semaphore_signal(barrier, inc=1, device_id=at(step), device_id_type=MESH)

    loads = [
        pltpu.make_async_copy(source, goal, held_sem.at[i])
        for i, (source, goal) in enumerate(zip(operands, held))
    ]
    for i in LOAD_ORDER:
        loads[i].start()

    def send(phase, back):
        for step, offset, rows, _ in slabs:
            goal = tuple(-s for s in step) if back else step
            pltpu.make_async_remote_copy(
                src_ref=send_buf.at[phase, pl.ds(offset, rows)],
                dst_ref=recv_buf.at[phase, pl.ds(offset, rows)],
                send_sem=send_sem.at[phase],
                recv_sem=recv_sem.at[phase],
                device_id=at(goal),
                device_id_type=MESH,
            ).start()

    def wait_in(phase):
        whole = recv_buf.at[phase]
        pltpu.make_async_copy(whole, whole, recv_sem.at[phase]).wait()

    def wait_out(phase):
        whole = send_buf.at[phase]
        pltpu.make_async_copy(whole, whole, send_sem.at[phase]).wait()

    lane = lax.broadcasted_iota(jnp.int32, (8, atoms), 1)
    sub = lax.broadcasted_iota(jnp.int32, (8, atoms), 0)
    low8 = lane < half
    few = 8 * cell_rows
    turns = (half, half, few)
    counts = (pairs, pairs, 2 * neighbours.shape[0] * few // (2 * atoms))
    spread = 4 * pairs

    def low_of(x):
        return lax.broadcasted_iota(jnp.int32, x.shape, 1) < half

    def turn(x):
        return pltpu.roll(x, half, 1)

    def fold(x, group):
        x = x + turn(x)
        return x + pltpu.roll(x, few, 1) if group == 2 else x

    def dup(x, group):
        if group == 0:
            return jnp.where(low_of(x), x, turn(x))
        return jnp.where(low_of(x), turn(x), x)

    def paired(x):
        top, bottom = x[:pairs], x[pairs:]
        return (
            jnp.where(low8, top, turn(bottom)),
            jnp.where(low8, turn(top), bottom),
        )

    for i in LOAD_ORDER[:9]:
        loads[i].wait()

    cell_ids = {}
    spot = sub % cell_rows
    cells = list(itertools.product((0, 1), repeat=3))
    for cell in cells:
        value = jnp.full((8, atoms), send_list[cell + (0,)], jnp.int32)
        for k in range(1, cell_rows):
            value = jnp.where(spot == k, send_list[cell + (k,)], value)
        cell_ids[cell] = value
    none = jnp.full((8, atoms), -1, jnp.int32)
    cell_ids[None] = none

    def place(cell, shift):
        return none if cell is None else cells.index(cell) * cell_rows + sub - shift

    row_ids, chosen, rep_one, rep_all = [], [], [], []
    within = lane % few
    for step, offset, rows, blocks in slabs:
        for cell_a, cell_b in blocks:
            ids = jnp.where(sub < cell_rows, cell_ids[cell_a], cell_ids[cell_b])
            chosen.append(jnp.where(ids == lane, 1.0, 0.0))
            spots = jnp.where(sub < cell_rows, place(cell_a, 0), place(cell_b, cell_rows))
            rep_one.append(jnp.where(spots == lane, 1.0, 0.0))
            rep_all.append(jnp.where(spots == within, 1.0, 0.0))
            base_a = ghost_row(step, cell_a, atoms, cell_rows) + sub
            if cell_b is None:
                base_b = none
            else:
                base_b = ghost_row(step, cell_b, atoms, cell_rows) + sub - cell_rows
            row_ids.append(jnp.where(sub < cell_rows, base_a, base_b))
    sel[...] = jnp.concatenate(chosen, axis=0).astype(BF16)
    rep[0] = jnp.concatenate(rep_one, axis=0).astype(BF16)
    rep[1] = jnp.concatenate(rep_all, axis=0).astype(BF16)
    boundary = []
    for i in range(0, 8, 2):
        ids = jnp.where(sub < cell_rows, cell_ids[cells[i]], cell_ids[cells[i + 1]])
        boundary.append(jnp.where(ids == lane, 1.0, 0.0))
    sel_b[...] = jnp.concatenate(boundary * (atoms // few), axis=0).astype(BF16)

    kinds = jnp.where(sub == jnp.broadcast_to(species[...], (8, atoms)), 1.0, 0.0).astype(BF16)
    emb_t = embedding[...].astype(F32).T.astype(BF16)
    start_t = dot(emb_t, kinds)
    start_b = start_t.astype(BF16)
    start_edge = dot_nt(start_b, sel_b[...])
    send_buf[0] = dot_nt(rep[0], start_edge.astype(BF16))

    for t in range(2):
        pad = jnp.zeros((8, hidden), F32)
        w_in[t * hidden : (t + 1) * hidden] = (
            jnp.concatenate([weight_rows(radial_in[t]), pad], axis=0).T.astype(BF16)
        )
        w_mid[t] = weight_rows(radial_mid[t]).T.astype(BF16)
        w_out[t] = weight_rows(radial_out[t]).T.astype(BF16)

    nbr_f = neighbours[...].astype(F32)
    raw = jnp.concatenate([vectors[0], vectors[1], vectors[2], nbr_f], axis=0)
    raw_high = raw.astype(BF16).astype(F32)
    raw_mid = (raw - raw_high).astype(BF16).astype(F32)
    pieces = jnp.concatenate([raw_high, raw_mid, raw - raw_high - raw_mid], axis=0)
    pieces = dot_nt(pieces.astype(BF16), sel_b[...])
    depth = raw.shape[0]
    edge_raw = pieces[:depth] + pieces[depth : 2 * depth] + pieces[2 * depth :]

    def quarters(x):
        rows = counts[2]
        out = x[:rows]
        for i in range(1, atoms // few):
            out = jnp.where(lane[:rows] // few == i, x[i * rows : (i + 1) * rows], out)
        return jnp.concatenate([out, out], axis=0)

    slots = neighbours.shape[0]
    edge_parts = [quarters(edge_raw[k * slots : (k + 1) * slots]) for k in range(4)]
    vec = [paired(vectors[k]) + (edge_parts[k],) for k in range(3)]
    nbr = paired(nbr_f) + (edge_parts[3],)
    geo = []
    for g in range(3):
        x, y, z = vec[0][g], vec[1][g], vec[2][g]
        length = jnp.sqrt(x * x + y * y + z * z)
        over = 1.0 / length
        nx, ny, nz = x * over, y * over, z * over
        geo.append((nx, ny, nz, over))
        u = length * (1.0 / CUTOFF)
        u2 = u * u
        u4 = u2 * u2
        u5 = u4 * u
        inside = u < 1.0
        env = 1.0 - 21.0 * u5 + 35.0 * u5 * u - 15.0 * u5 * u2
        denv = (-105.0 / CUTOFF) * u4 * (1.0 - u) * (1.0 - u)
        cut[g, 0] = jnp.where(inside, 0.25 * env, 0.0)
        cut[g, 1] = jnp.where(inside, 0.25 * denv, 0.0)
        theta = PI * u
        sin1, cos1 = jnp.sin(theta), jnp.cos(theta)
        twice = 2.0 * cos1
        s_old, s_now = jnp.zeros_like(sin1), sin1
        c_old, c_now = jnp.ones_like(cos1), cos1
        amp0 = (2.0 / CUTOFF) ** 0.5
        for k in range(1, 9):
            base = amp0 * s_now * over
            slope = (amp0 * k * PI / CUTOFF * c_now - base) * over
            basis[g, 0, (k - 1) * 8 : k * 8] = base
            basis[g, 1, (k - 1) * 8 : k * 8] = slope
            s_old, s_now = s_now, twice * s_now - s_old
            c_old, c_now = c_now, twice * c_now - c_old
        ylm = (
            ROOT3 * nx,
            ROOT3 * ny,
            ROOT3 * nz,
            ROOT15 * nx * ny,
            ROOT15 * ny * nz,
            0.5 * ROOT5 * (3.0 * nz * nz - 1.0),
            ROOT15 * nx * nz,
            0.5 * ROOT15 * (nx * nx - ny * ny),
        )
        for m in range(8):
            for p in range(counts[g]):
                harm[g * pairs + p, m * 8 : (m + 1) * 8] = jnp.broadcast_to(
                    ylm[m][p : p + 1], (8, atoms)
                )

    own_rows = jnp.concatenate([sub + 8 * b for b in range(atoms // 8)], axis=0).astype(F32)
    all_rows = jnp.concatenate([own_rows] + [r.astype(F32) for r in row_ids], axis=0)
    onehots = (oh_own, oh_ghost, oh_edge)

    def onehot(g):
        ids = own_rows if g == 0 else all_rows
        for p in range(counts[g]):
            onehots[g][:, p * atoms : (p + 1) * atoms] = jnp.where(
                ids == nbr[g][p : p + 1], 1.0, 0.0
            ).astype(BF16)

    def silu_pair(x, dx):
        gate = 0.5 + 0.5 * jnp.tanh(0.5 * x)
        value = x * gate
        return value, gate * (1.0 + x - value) * dx

    def tiles(t, g):
        return spread if g == 2 else (t * 2 + g) * pairs

    def radial(g, layers):
        top = layers[-1] * hidden + hidden

        def chunk(j):
            def wide(kind):
                return jnp.concatenate(
                    [basis[g, kind, pl.ds(2 * j + i, 8, stride=8), :] for i in range(2)], axis=1
                )

            def row(kind):
                return jnp.concatenate(
                    [cut[g, kind, 2 * j + i : 2 * j + i + 1, :] for i in range(2)], axis=1
                )

            env, denv = row(0), row(1)

            def first_dot(x):
                high = x.astype(BF16).astype(F32)
                full = jnp.concatenate([high, x - high, high, jnp.zeros_like(x)], axis=0)
                return dot(w_in[:top], full.astype(BF16))

            one, done = silu_pair(first_dot(wide(0)), first_dot(wide(1)))
            for t in layers:
                rows = slice(t * hidden, (t + 1) * hidden)
                two, dtwo = silu_pair(
                    dot(w_mid[t], split_rows(one[rows])), dot(w_mid[t], split_rows(done[rows]))
                )
                value = dot(w_out[t], split_rows(env * two))
                slope = dot(w_out[t], split_rows(denv * two + env * dtwo))
                for i in range(2):
                    lanes = slice(i * atoms, (i + 1) * atoms)
                    rad[tiles(t, g) + 2 * j + i] = value[:, lanes]
                    drad[tiles(t, g) + 2 * j + i] = slope[:, lanes]

        loop(counts[g] // 2, chunk)

    def gather(t, g, own_t, ghost_t):
        for j in range(counts[g] // 2):
            lanes = slice(j * 2 * atoms, (j + 1) * 2 * atoms)
            out = dot(own_t, onehots[g][:atoms, lanes])
            if g > 0:
                out = out + dot(ghost_t, onehots[g][atoms:, lanes])
            feat[tiles(t, g) + 2 * j] = out[:, :atoms]
            feat[tiles(t, g) + 2 * j + 1] = out[:, atoms:]

    def twin(y):
        return jnp.concatenate([y, y], axis=0)

    def forward(t, g):
        which = 4 if g == 2 else t * 2 + g
        base = tiles(t, g)
        parts_out = ([], [], [])
        for c in range(0, channels, 16):
            total = [jnp.zeros((16, atoms), F32) for _ in range(9)]
            for p in range(counts[g]):
                v = feat[base + p, c : c + 16]
                parts = [
                    rad[base + p, l * channels + c : l * channels + c + 16] * v for l in range(3)
                ]
                total[0] = total[0] + parts[0]
                for m in range(8):
                    y = twin(harm[g * pairs + p, m * 8 : (m + 1) * 8])
                    total[1 + m] = total[1 + m] + y * parts[1 if m < 3 else 2]
            total = [fold(a, g) for a in total]
            for m in range(1, 9):
                amp[which, m, c : c + 16] = total[m]
            parts_out[0].append(total[0])
            parts_out[1].append(sum(a * a for a in total[1:4]))
            parts_out[2].append(sum(a * a for a in total[4:9]))
        return jnp.concatenate(parts_out[0] + parts_out[1] + parts_out[2], axis=0)

    def backward(t, g, dinv, adding):
        which = 4 if g == 2 else t * 2 + g
        base = tiles(t, g)
        for c in range(0, channels, 16):
            rows = slice(c, c + 16)
            amp[which, 0, rows] = dinv[rows]
            d1 = 2.0 * dinv[channels + c : channels + c + 16]
            d2 = 2.0 * dinv[2 * channels + c : 2 * channels + c + 16]
            for m in range(1, 9):
                amp[which, m, rows] = amp[which, m, rows] * (d1 if m < 4 else d2)
        for p in range(counts[g]):
            ys = [twin(harm[g * pairs + p, m * 8 : (m + 1) * 8]) for m in range(8)]
            total = [jnp.zeros((16, atoms), F32) for _ in range(9)]
            for c in range(0, channels, 16):
                rows = slice(c, c + 16)
                v = feat[base + p, rows]
                r = [rad[base + p, l * channels + c : l * channels + c + 16] for l in range(3)]
                q = [drad[base + p, l * channels + c : l * channels + c + 16] for l in range(3)]
                d = [amp[which, m, rows] for m in range(9)]
                t1 = ys[0] * d[1] + ys[1] * d[2] + ys[2] * d[3]
                t2 = ys[3] * d[4] + ys[4] * d[5] + ys[5] * d[6] + ys[6] * d[7] + ys[7] * d[8]
                if t == 1:
                    cot_feat[g, rows, p * atoms : (p + 1) * atoms] = (
                        r[0] * d[0] + r[1] * t1 + r[2] * t2
                    ).astype(BF16)
                total[0] = total[0] + v * (q[0] * d[0] + q[1] * t1 + q[2] * t2)
                p1, p2 = v * r[1], v * r[2]
                for m in range(1, 9):
                    total[m] = total[m] + (p1 if m < 4 else p2) * d[m]
            for m in range(9):
                part = total[m][:8] + total[m][8:]
                spots = slice(p * 8, (p + 1) * 8)
                if adding:
                    part = part + acc_ref[g, m, spots]
                acc_ref[g, m, spots] = part

    def edge_grads(g):
        n = counts[g]
        d = []
        for m in range(9):
            d.append(sum(acc_ref[g, m, pl.ds(j, n, stride=8), :] for j in range(8)))
        nx, ny, nz, over = [v[:n] for v in geo[g]]
        gx = ROOT3 * d[1] + ROOT15 * (ny * d[4] + nz * d[7] + nx * d[8])
        gy = ROOT3 * d[2] + ROOT15 * (nx * d[4] + nz * d[5] - ny * d[8])
        gz = ROOT3 * d[3] + ROOT15 * (ny * d[5] + nx * d[7]) + (3.0 * ROOT5) * nz * d[6]
        along = d[0] - (nx * gx + ny * gy + nz * gz) * over
        grad = [a * along + b * over for a, b in ((nx, gx), (ny, gy), (nz, gz))]
        basis[g, 0, 0:64] = jnp.zeros((64, atoms), F32)
        for k in range(3):
            basis[g, 0, k * 8 : k * 8 + n] = -grad[k]
        for p in range(n):
            row = basis[g, 0, pl.ds(p, 8, stride=8), :]
            high = row.astype(BF16).astype(F32)
            grad_cat[g, :, p * atoms : (p + 1) * atoms] = jnp.concatenate(
                [high, row - high], axis=0
            ).astype(BF16)
        return [fold(jnp.sum(v, axis=0, keepdims=True), g) for v in grad]

    onehot(2)
    radial(2, (0,))
    onehot(0)
    onehot(1)
    radial(0, (0, 1))
    pl.semaphore_wait(barrier, len(slabs))
    send(0, False)
    radial(1, (0, 1))
    for i in LOAD_ORDER[9:]:
        loads[i].wait()
    mix_t[...] = weight_rows(mixing[0]).T.astype(BF16)
    high = mixing[0].astype(BF16).astype(F32)
    mix_c[...] = jnp.concatenate([high, high, mixing[0] - high], axis=1).astype(BF16)
    rl_col = jnp.broadcast_to(read_linear[...], (channels, channels)).T
    rh = read_hidden[...]
    rh_high = rh.astype(BF16).astype(F32)
    rh_two = jnp.concatenate([rh_high, rh - rh_high], axis=1).astype(BF16)
    rh_t = jnp.concatenate([rh_high, rh_high, rh - rh_high], axis=1).astype(BF16)
    rh_c = weight_rows(rh).T.astype(BF16)
    ro_col = jnp.broadcast_to(read_out[...], (channels, read_out.shape[1])).T
    high = mixing[1].astype(BF16).astype(F32)
    mixed = dot_nt(
        rh_t, jnp.concatenate([high, mixing[1] - high, high], axis=1).astype(BF16)
    )
    high = mixed.astype(BF16).astype(F32)
    act_w = jnp.concatenate([high, high, mixed - high], axis=1).astype(BF16)
    dact_w = weight_rows(mixed).T.astype(BF16)
    gather(0, 0, start_b, None)
    inv_own = forward(0, 0)

    wait_in(0)
    ghost_t = recv_buf[0].T.astype(BF16)
    gather(0, 2, start_b, ghost_t)
    first_edge = start_edge + dot(mix_t[...], split_rows(forward(0, 2)))
    send_buf[1] = dot_nt(rep[0], first_edge.astype(BF16))
    send(1, False)
    gather(0, 1, start_b, ghost_t)
    inv_both = jnp.where(low_of(inv_own), inv_own, forward(0, 1))
    first_b = (start_t + dot(mix_t[...], split_rows(inv_both))).astype(BF16)
    first_ref[...] = first_b.astype(F32)

    def energy_own(g):
        own = dup(first_ref[...], g)
        doubled = jnp.concatenate([own, own], axis=0).astype(BF16)
        return jnp.sum(rl_col * own, axis=0, keepdims=True), dot(rh_two, doubled)

    def energy(features, site, act):
        act = act + dot(act_w, split_rows(features))
        gate = 0.5 + 0.5 * jnp.tanh(0.5 * act)
        value = act * gate
        site = site + jnp.sum(ro_col * value, axis=0, keepdims=True)
        dact = split_rows(ro_col * gate * (1.0 + act - value))
        return site, dact, dot(dact_w, dact)

    gather(1, 0, first_b, None)
    site_own, dact_own, dinv = energy(forward(1, 0), *energy_own(0))
    backward(1, 0, dinv, False)
    before = energy_own(1)
    wait_in(1)
    gather(1, 1, first_b, recv_buf[1].T.astype(BF16))
    site_ghost, dact_ghost, dinv = energy(forward(1, 1), *before)
    backward(1, 1, dinv, False)
    send_buf[2] = dot_nt(oh_ghost[atoms:], cot_feat[1])
    send(2, True)
    site_out[...] = jnp.where(low_of(site_own), site_own, site_ghost)

    cot_own, cot_ghost = dot(rh_c, dact_own), dot(rh_c, dact_ghost)
    cot = rl_col + jnp.where(low_of(cot_own), cot_own, cot_ghost)
    cot = cot + dot_nt(cot_feat[0], oh_own[...]) + dot_nt(cot_feat[1], oh_ghost[:atoms])
    sums = []
    for g in range(2):
        backward(0, g, dot(mix_c[...], split_rows(dup(cot, g))), True)
        sums.append(edge_grads(g))
    outward = dot_nt(oh_ghost[atoms:], grad_cat[1])
    local = dot_nt(grad_cat[0], oh_own[...]) + dot_nt(grad_cat[1], oh_ghost[:atoms])
    mine = jnp.concatenate(
        [jnp.where(low_of(sums[0][k]), sums[0][k], sums[1][k]) for k in range(3)], axis=0
    )
    local = local[:3] + local[8:11] + mine
    send_buf[3] = jnp.zeros((ghosts, atoms), F32)

    wait_in(2)
    back = recv_buf[2].T
    high = back.astype(BF16).astype(F32)
    parts = dot(jnp.concatenate([high, back - high], axis=0).astype(BF16), rep[1])
    dinv = dot(mix_c[...], split_rows(parts[:channels] + parts[channels:]))
    backward(0, 2, dinv, False)
    sums = edge_grads(2)
    width = counts[2] * atoms
    send_buf[3, :, 0:16] = outward + dot_nt(oh_edge[atoms:], grad_cat[2, :, :width])
    send(3, True)
    parts = dot_nt(grad_cat[2, :, :width], oh_edge[:atoms])
    local = local + parts[:3] + parts[8:11]
    rows = jnp.concatenate(sums + [jnp.zeros((5, atoms), F32)], axis=0)
    rows = jnp.where(lane < few, rows, 0.0)

    def exact(x, chooser):
        high = x.astype(BF16).astype(F32)
        mid = (x - high).astype(BF16).astype(F32)
        out = dot(jnp.concatenate([high, mid, x - high - mid], axis=0).astype(BF16), chooser)
        return out[:3] + out[8:11] + out[16:19]

    local = local + exact(rows, sel_b[...])
    wait_in(3)
    back = recv_buf[3].T
    force_out[...] = local + exact(back[:8] + back[8:16], sel[...])
    for phase in range(4):
        wait_out(phase)


def finish(site_in, force_in, site_out, force_out):
    site_out[...] = site_in[0]
    force_out[...] = force_in[...]


def solution(mesh):
    sizes = tuple(mesh.shape[axis] for axis in AXES)

    def body(
        species,
        send_list,
        neighbours,
        edge_vectors,
        embedding,
        radial_in,
        radial_mid,
        radial_out,
        mixing,
        read_linear,
        read_hidden,
        read_out,
    ):
        atoms = species.shape[0]
        channels = embedding.shape[1]
        slots = neighbours.shape[0]
        pairs = slots // 2
        hidden = radial_mid.shape[1]
        ghosts = plan_slabs(send_list.shape[3])[1]
        vmem = pl.BlockSpec(memory_space=pltpu.VMEM)
        operands = (
            species.reshape(1, atoms),
            send_list,
            neighbours,
            edge_vectors,
            embedding,
            radial_in,
            radial_mid,
            radial_out,
            mixing,
            read_linear.reshape(1, channels),
            read_hidden.T,
            read_out.reshape(1, read_out.shape[0]),
        )
        site, forces = pl.pallas_call(
            functools.partial(kernel, sizes),
            out_shape=(pltpu.VMEM((1, atoms), F32), pltpu.VMEM((3, atoms), F32)),
            in_specs=[tuple(pl.BlockSpec(memory_space=pltpu.HBM) for _ in operands)],
            out_specs=(vmem, vmem),
            scratch_shapes=[
                pltpu.VMEM((3, 2, 8 * pairs, atoms), F32),
                pltpu.VMEM((3, 2, pairs, atoms), F32),
                pltpu.VMEM((3 * pairs, 64, atoms), F32),
                pltpu.VMEM((5 * pairs, 3 * channels, atoms), F32),
                pltpu.VMEM((5 * pairs, 3 * channels, atoms), F32),
                pltpu.VMEM((atoms, pairs * atoms), BF16),
                pltpu.VMEM((atoms + ghosts, pairs * atoms), BF16),
                pltpu.VMEM((atoms + ghosts, pairs * atoms // 2), BF16),
                pltpu.VMEM((5 * pairs, channels, atoms), F32),
                pltpu.VMEM((5, 9, channels, atoms), F32),
                pltpu.VMEM((2, channels, pairs * atoms), BF16),
                pltpu.VMEM((3, 9, 8 * pairs, atoms), F32),
                pltpu.VMEM((3, 16, pairs * atoms), BF16),
                pltpu.VMEM((ghosts, atoms), BF16),
                pltpu.VMEM((atoms, atoms), BF16),
                pltpu.VMEM((2, ghosts, atoms), BF16),
                pltpu.VMEM((2 * hidden, 32), BF16),
                pltpu.VMEM((2, hidden, 3 * hidden), BF16),
                pltpu.VMEM((2, 3 * channels, 3 * hidden), BF16),
                pltpu.VMEM((channels, 9 * channels), BF16),
                pltpu.VMEM((3 * channels, 3 * channels), BF16),
                pltpu.VMEM((channels, atoms), F32),
                pltpu.VMEM((4, ghosts, channels), F32),
                pltpu.VMEM((4, ghosts, channels), F32),
                pltpu.SemaphoreType.DMA((4,)),
                pltpu.SemaphoreType.DMA((4,)),
                tuple(
                    (pltpu.SMEM if x is send_list else pltpu.VMEM)(x.shape, x.dtype)
                    for x in operands
                ),
                pltpu.SemaphoreType.DMA((len(operands),)),
            ],
            compiler_params=pltpu.CompilerParams(
                collective_id=0, has_side_effects=True, vmem_limit_bytes=56 * 1024 * 1024
            ),
        )(operands)
        site, forces = [pltpu.with_memory_space_constraint(x, pltpu.VMEM) for x in (site, forces)]
        return pl.pallas_call(
            finish,
            out_shape=(
                jax.ShapeDtypeStruct((atoms,), F32),
                jax.ShapeDtypeStruct((3, atoms), F32),
            ),
            in_specs=[vmem, vmem],
            out_specs=(vmem, vmem),
        )(site, forces)

    in_specs = (
        P(AXES),
        P("gx", "gy", "gz", None),
        P(None, AXES),
        P(None, None, AXES),
        P(),
        P(),
        P(),
        P(),
        P(),
        P(),
        P(),
        P(),
    )
    out_specs = (P(AXES), P(None, AXES))
    return jax.shard_map(body, mesh=mesh, in_specs=in_specs, out_specs=out_specs, check_vma=False)
```

time: 43.2 us -> 39.6 us (0.917)
  Pallas kernels: 40.7 us -> 38.9 us
  local copies, waits for them, and re-layouts: 1.71 us -> 0 us
    pallas_call x1 -> x2, Pallas kernels: 40.7 us -> 38.9 us  [the longest x1 38.3 us: body(): pl.pallas_call(functools.partial(kernel, sizes), out_shape=(pltpu.VMEM((1...]
    unnamed x6 -> x0, local copies, waits for them, and re-layouts: 1.71 us -> none
where the time goes in v2:
time: 39.6 us; the launch traced here: 39.5 us
  Pallas kernels  38.9 us (98%)
  between operations  0.64 us (2%)
    pallas_call x1, Pallas kernels, body(): pl.pallas_call(functools.partial(kernel, sizes), out_shape=(pltpu.VMEM((1...  38.3 us

profile of v2, /device:TPU:1, one launch (start us, length us, event | category | flops | bytes accessed | tf_op | source)
XLA Modules:
  0.0 39.5 jit_solution(17907288335433258526)
XLA Ops:
  0.6 38.3 %shard_map.131 = (f32[1,128]{1,0:T(1,128)S(1)}, f32[3,128]{1,0:T(4,128)S(1)}) custom-call(s32[1,128]{1,0:T(1,128)} %bitcast.5, s32[2,2,2,4]{3,2,1,0:T(2,128)} %operands_1_.1, s32[16,128]{1,0:T(8,128)} %operands_2_.1, f32[3,16,128]{2,1,0:T(8,128)} %operands_3_.1, bf16[8,128]{1,0:T(8,128)(2,1)} %operands_4_.1, f32[2,8,64]{2,1,0:T(8,128)} %operands_5_.1, ...), custom_call_target="tpu_custom_call" | custom-call | tf_op jit(solution)/shard_map/pallas_call | solution.py:616
  38.9 0.6 %shard_map.132 = (f32[128]{0:T(128)}, f32[3,128]{1,0:T(4,128)}) custom-call(f32[1,128]{1,0:T(1,128)S(1)} %get-tuple-element.4.site_in, f32[3,128]{1,0:T(4,128)S(1)} %get-tuple-element.5.force_in), custom_call_target="tpu_custom_call" | custom-call | tf_op jit(solution)/shard_map/pallas_call | solution.py:659

commit v3 on v2

--- a/solution.py
+++ b/solution.py
@@ -17,6 +17,7 @@
 ROOT5 = 5.0**0.5
 ROOT15 = 15.0**0.5
 PI = 3.141592653589793
+WIDE = 8
 LOAD_ORDER = (1, 0, 4, 2, 3, 5, 6, 7, 9, 8, 10, 11)
 
 
@@ -99,6 +100,8 @@
     recv_buf,
     send_sem,
     recv_sem,
+    part,
+    edge_jac,
     held,
     held_sem,
 ):
@@ -123,6 +126,10 @@
     cell_rows = send_list.shape[3]
     hidden = radial_mid.shape[1]
     slabs, ghosts = plan_slabs(cell_rows)
+    ways = []
+    for step, _, _, _ in slabs:
+        kind = sum(s != 0 for s in step) - 1
+        ways.append((kind, sum(way[0] == kind for way in ways), step))
     me = [lax.axis_index(axis) for axis in AXES]
 
     def at(step):
@@ -142,24 +149,47 @@
         loads[i].start()
 
     def send(phase, back):
-        for step, offset, rows, _ in slabs:
+        for kind, index, step in ways:
             goal = tuple(-s for s in step) if back else step
             pltpu.make_async_remote_copy(
-                src_ref=send_buf.at[phase, pl.ds(offset, rows)],
-                dst_ref=recv_buf.at[phase, pl.ds(offset, rows)],
-                send_sem=send_sem.at[phase],
-                recv_sem=recv_sem.at[phase],
+                src_ref=send_buf[kind].at[phase, index],
+                dst_ref=recv_buf[kind].at[phase, index],
+                send_sem=send_sem.at[phase, kind],
+                recv_sem=recv_sem.at[phase, kind],
                 device_id=at(goal),
                 device_id_type=MESH,
             ).start()
 
+    def wait_all(bufs, sems, phase):
+        for kind, buf in enumerate(bufs):
+            whole = buf.at[phase]
+            pltpu.make_async_copy(whole, whole, sems.at[phase, kind]).wait()
+
     def wait_in(phase):
-        whole = recv_buf.at[phase]
-        pltpu.make_async_copy(whole, whole, recv_sem.at[phase]).wait()
+        wait_all(recv_buf, recv_sem, phase)
 
     def wait_out(phase):
-        whole = send_buf.at[phase]
-        pltpu.make_async_copy(whole, whole, send_sem.at[phase]).wait()
+        wait_all(send_buf, send_sem, phase)
+
+    def fill(phase, rows):
+        start = 0
+        for buf in send_buf:
+            count, depth = buf.shape[1:3]
+            part_rows = rows[start : start + count * depth]
+            buf[phase, :, :, : rows.shape[1]] = part_rows.reshape(
+                count, depth, rows.shape[1]
+            ).astype(BF16)
+            start += count * depth
+
+    def arrived(phase):
+        parts = []
+        for buf in recv_buf:
+            block = buf[phase]
+            count, depth, width = block.shape
+            if depth % 16:
+                block = block.astype(F32).reshape(count * depth, width).astype(BF16)
+            parts.append(block.reshape(count * depth, width))
+        return jnp.concatenate(parts, axis=0).T
 
     lane = lax.broadcasted_iota(jnp.int32, (8, atoms), 1)
     sub = lax.broadcasted_iota(jnp.int32, (8, atoms), 0)
@@ -191,7 +221,7 @@
             jnp.where(low8, turn(top), bottom),
         )
 
-    for i in LOAD_ORDER[:9]:
+    for i in LOAD_ORDER:
         loads[i].wait()
 
     cell_ids = {}
@@ -237,7 +267,7 @@
     start_t = dot(emb_t, kinds)
     start_b = start_t.astype(BF16)
     start_edge = dot_nt(start_b, sel_b[...])
-    send_buf[0] = dot_nt(rep[0], start_edge.astype(BF16))
+    fill(0, dot_nt(rep[0], start_edge.astype(BF16)))
 
     for t in range(2):
         pad = jnp.zeros((8, hidden), F32)
@@ -335,15 +365,15 @@
         top = layers[-1] * hidden + hidden
 
         def chunk(j):
+            spots = range(j * WIDE, min(counts[g], (j + 1) * WIDE))
+
             def wide(kind):
                 return jnp.concatenate(
-                    [basis[g, kind, pl.ds(2 * j + i, 8, stride=8), :] for i in range(2)], axis=1
+                    [basis[g, kind, pl.ds(p, 8, stride=8), :] for p in spots], axis=1
                 )
 
             def row(kind):
-                return jnp.concatenate(
-                    [cut[g, kind, 2 * j + i : 2 * j + i + 1, :] for i in range(2)], axis=1
-                )
+                return jnp.concatenate([cut[g, kind, p : p + 1, :] for p in spots], axis=1)
 
             env, denv = row(0), row(1)
 
@@ -360,21 +390,25 @@
                 )
                 value = dot(w_out[t], split_rows(env * two))
                 slope = dot(w_out[t], split_rows(denv * two + env * dtwo))
-                for i in range(2):
+                for i, p in enumerate(spots):
                     lanes = slice(i * atoms, (i + 1) * atoms)
-                    rad[tiles(t, g) + 2 * j + i] = value[:, lanes]
-                    drad[tiles(t, g) + 2 * j + i] = slope[:, lanes]
-
-        loop(counts[g] // 2, chunk)
-
-    def gather(t, g, own_t, ghost_t):
+                    rad[tiles(t, g) + p] = value[:, lanes]
+                    drad[tiles(t, g) + p] = slope[:, lanes]
+
+        loop(-(-counts[g] // WIDE), chunk)
+
+    def gather(t, g, rows_t, ghosts_too=False):
         for j in range(counts[g] // 2):
             lanes = slice(j * 2 * atoms, (j + 1) * 2 * atoms)
-            out = dot(own_t, onehots[g][:atoms, lanes])
-            if g > 0:
-                out = out + dot(ghost_t, onehots[g][atoms:, lanes])
-            feat[tiles(t, g) + 2 * j] = out[:, :atoms]
-            feat[tiles(t, g) + 2 * j + 1] = out[:, atoms:]
+            first, second = tiles(t, g) + 2 * j, tiles(t, g) + 2 * j + 1
+            if ghosts_too:
+                out = dot(rows_t, onehots[g][atoms:, lanes])
+                feat[first] = feat[first] + out[:, :atoms]
+                feat[second] = feat[second] + out[:, atoms:]
+            else:
+                out = dot(rows_t, onehots[g][:atoms, lanes])
+                feat[first] = out[:, :atoms]
+                feat[second] = out[:, atoms:]
 
     def twin(y):
         return jnp.concatenate([y, y], axis=0)
@@ -423,7 +457,7 @@
                 d = [amp[which, m, rows] for m in range(9)]
                 t1 = ys[0] * d[1] + ys[1] * d[2] + ys[2] * d[3]
                 t2 = ys[3] * d[4] + ys[4] * d[5] + ys[5] * d[6] + ys[6] * d[7] + ys[7] * d[8]
-                if t == 1:
+                if t == 1 and g == 0:
                     cot_feat[g, rows, p * atoms : (p + 1) * atoms] = (
                         r[0] * d[0] + r[1] * t1 + r[2] * t2
                     ).astype(BF16)
@@ -432,21 +466,88 @@
                 for m in range(1, 9):
                     total[m] = total[m] + (p1 if m < 4 else p2) * d[m]
             for m in range(9):
-                part = total[m][:8] + total[m][8:]
+                whole = total[m][:8] + total[m][8:]
                 spots = slice(p * 8, (p + 1) * 8)
                 if adding:
-                    part = part + acc_ref[g, m, spots]
-                acc_ref[g, m, spots] = part
+                    whole = whole + acc_ref[g, m, spots]
+                acc_ref[g, m, spots] = whole
+
+    def early_cot():
+        base = tiles(1, 1)
+        for p in range(pairs):
+            ys = [twin(harm[pairs + p, m * 8 : (m + 1) * 8]) for m in range(8)]
+            for c in range(0, channels, 16):
+                a = [amp[3, m, c : c + 16] for m in range(1, 9)]
+                t1 = ys[0] * a[0] + ys[1] * a[1] + ys[2] * a[2]
+                t2 = ys[3] * a[3] + ys[4] * a[4] + ys[5] * a[5] + ys[6] * a[6] + ys[7] * a[7]
+                for l, t in ((1, t1), (2, t2)):
+                    at_l = l * channels + c
+                    at_s = at_l - channels
+                    part[p, at_s : at_s + 16] = rad[base + p, at_l : at_l + 16] * t
+
+    def late_cot(dinv):
+        base = tiles(1, 1)
+        for c in range(0, channels, 16):
+            d0 = dinv[c : c + 16]
+            d1 = 2.0 * dinv[channels + c : channels + c + 16]
+            d2 = 2.0 * dinv[2 * channels + c : 2 * channels + c + 16]
+            for p in range(pairs):
+                cot_feat[1, c : c + 16, p * atoms : (p + 1) * atoms] = (
+                    rad[base + p, c : c + 16] * d0
+                    + part[p, c : c + 16] * d1
+                    + part[p, channels + c : channels + c + 16] * d2
+                ).astype(BF16)
+
+    def slopes():
+        base = tiles(0, 2)
+        for p in range(counts[2]):
+            ys = [twin(harm[2 * pairs + p, m * 8 : (m + 1) * 8]) for m in range(8)]
+            for c in range(0, channels, 16):
+                v = 2.0 * feat[base + p, c : c + 16]
+                r = [rad[base + p, l * channels + c : l * channels + c + 16] for l in range(3)]
+                q = [drad[base + p, l * channels + c : l * channels + c + 16] for l in range(3)]
+                a = [amp[4, m, c : c + 16] for m in range(1, 9)]
+                t1 = ys[0] * a[0] + ys[1] * a[1] + ys[2] * a[2]
+                t2 = ys[3] * a[3] + ys[4] * a[4] + ys[5] * a[5] + ys[6] * a[6] + ys[7] * a[7]
+                p1, p2 = ROOT3 * (v * r[1]), ROOT5 * (v * r[2])
+                out = (
+                    0.5 * v * q[0],
+                    v * q[1] * t1,
+                    v * q[2] * t2,
+                    p1 * a[0],
+                    p1 * a[1],
+                    p1 * a[2],
+                    p2 * (ys[1] * a[3] + ys[2] * a[6] + ys[0] * a[7]),
+                    p2 * (ys[0] * a[3] + ys[2] * a[4] - ys[1] * a[7]),
+                    p2 * (ys[1] * a[4] + ys[0] * a[6] + ROOT3 * (ys[2] * a[5])),
+                )
+                for i, x in enumerate(out):
+                    edge_jac[p, i, c : c + 16] = x
+
+    def edge_backward(dinv):
+        for p in range(counts[2]):
+            total = [jnp.zeros((16, atoms), F32) for _ in range(4)]
+            for c in range(0, channels, 16):
+                d = [dinv[l * channels + c : l * channels + c + 16] for l in range(3)]
+                x = [edge_jac[p, i, c : c + 16] for i in range(9)]
+                total[0] = total[0] + (x[0] * d[0] + x[1] * d[1] + x[2] * d[2])
+                for k in range(3):
+                    total[1 + k] = total[1 + k] + (x[3 + k] * d[1] + x[6 + k] * d[2])
+            for m in range(4):
+                acc_ref[2, m, p * 8 : (p + 1) * 8] = total[m][:8] + total[m][8:]
 
     def edge_grads(g):
         n = counts[g]
         d = []
-        for m in range(9):
+        for m in range(4 if g == 2 else 9):
             d.append(sum(acc_ref[g, m, pl.ds(j, n, stride=8), :] for j in range(8)))
         nx, ny, nz, over = [v[:n] for v in geo[g]]
-        gx = ROOT3 * d[1] + ROOT15 * (ny * d[4] + nz * d[7] + nx * d[8])
-        gy = ROOT3 * d[2] + ROOT15 * (nx * d[4] + nz * d[5] - ny * d[8])
-        gz = ROOT3 * d[3] + ROOT15 * (ny * d[5] + nx * d[7]) + (3.0 * ROOT5) * nz * d[6]
+        if g == 2:
+            gx, gy, gz = d[1:]
+        else:
+            gx = ROOT3 * d[1] + ROOT15 * (ny * d[4] + nz * d[7] + nx * d[8])
+            gy = ROOT3 * d[2] + ROOT15 * (nx * d[4] + nz * d[5] - ny * d[8])
+            gz = ROOT3 * d[3] + ROOT15 * (ny * d[5] + nx * d[7]) + (3.0 * ROOT5) * nz * d[6]
         along = d[0] - (nx * gx + ny * gy + nz * gz) * over
         grad = [a * along + b * over for a, b in ((nx, gx), (ny, gy), (nz, gz))]
         basis[g, 0, 0:64] = jnp.zeros((64, atoms), F32)
@@ -455,24 +556,38 @@
         for p in range(n):
             row = basis[g, 0, pl.ds(p, 8, stride=8), :]
             high = row.astype(BF16).astype(F32)
-            grad_cat[g, :, p * atoms : (p + 1) * atoms] = jnp.concatenate(
-                [high, row - high], axis=0
-            ).astype(BF16)
+            both = jnp.concatenate([high, row - high], axis=0).astype(BF16)
+            lanes = slice(p * atoms, (p + 1) * atoms)
+            grad_cat[g, 0:16, lanes] = both
+            grad_cat[g, 16:32, lanes] = both
         return [fold(jnp.sum(v, axis=0, keepdims=True), g) for v in grad]
 
+    pl.semaphore_wait(barrier, len(slabs))
+    send(0, False)
     onehot(2)
     radial(2, (0,))
+    gather(0, 2, start_b)
+    mix_t[...] = weight_rows(mixing[0]).T.astype(BF16)
+    onehot(1)
+    radial(1, (0, 1))
+    gather(0, 1, start_b)
     onehot(0)
-    onehot(1)
-    radial(0, (0, 1))
-    pl.semaphore_wait(barrier, len(slabs))
-    send(0, False)
-    radial(1, (0, 1))
-    for i in LOAD_ORDER[9:]:
-        loads[i].wait()
-    mix_t[...] = weight_rows(mixing[0]).T.astype(BF16)
-    high = mixing[0].astype(BF16).astype(F32)
-    mix_c[...] = jnp.concatenate([high, high, mixing[0] - high], axis=1).astype(BF16)
+    radial(0, (0,))
+    gather(0, 0, start_b)
+
+    wait_in(0)
+    ghost_t = arrived(0)
+    gather(0, 2, ghost_t, True)
+    first_edge = start_edge + dot(mix_t[...], split_rows(forward(0, 2)))
+    fill(1, dot_nt(rep[0], first_edge.astype(BF16)))
+    send(1, False)
+    gather(0, 1, ghost_t, True)
+    inv_own = forward(0, 0)
+    inv_both = jnp.where(low_of(inv_own), inv_own, forward(0, 1))
+    first_b = (start_t + dot(mix_t[...], split_rows(inv_both))).astype(BF16)
+    first_ref[...] = first_b.astype(F32)
+    gather(1, 1, first_b)
+
     rl_col = jnp.broadcast_to(read_linear[...], (channels, channels)).T
     rh = read_hidden[...]
     rh_high = rh.astype(BF16).astype(F32)
@@ -487,19 +602,6 @@
     high = mixed.astype(BF16).astype(F32)
     act_w = jnp.concatenate([high, high, mixed - high], axis=1).astype(BF16)
     dact_w = weight_rows(mixed).T.astype(BF16)
-    gather(0, 0, start_b, None)
-    inv_own = forward(0, 0)
-
-    wait_in(0)
-    ghost_t = recv_buf[0].T.astype(BF16)
-    gather(0, 2, start_b, ghost_t)
-    first_edge = start_edge + dot(mix_t[...], split_rows(forward(0, 2)))
-    send_buf[1] = dot_nt(rep[0], first_edge.astype(BF16))
-    send(1, False)
-    gather(0, 1, start_b, ghost_t)
-    inv_both = jnp.where(low_of(inv_own), inv_own, forward(0, 1))
-    first_b = (start_t + dot(mix_t[...], split_rows(inv_both))).astype(BF16)
-    first_ref[...] = first_b.astype(F32)
 
     def energy_own(g):
         own = dup(first_ref[...], g)
@@ -514,60 +616,65 @@
         dact = split_rows(ro_col * gate * (1.0 + act - value))
         return site, dact, dot(dact_w, dact)
 
-    gather(1, 0, first_b, None)
+    before = energy_own(1)
+    wait_in(1)
+    gather(1, 1, arrived(1), True)
+    features = forward(1, 1)
+    early_cot()
+    site_ghost, dact_ghost, dinv_ghost = energy(features, *before)
+    late_cot(dinv_ghost)
+    fill(2, dot_nt(oh_ghost[atoms:], cot_feat[1]))
+    send(2, True)
+
+    slopes()
+    high = mixing[0].astype(BF16).astype(F32)
+    mix_c[...] = jnp.concatenate([high, high, mixing[0] - high], axis=1).astype(BF16)
+    radial(0, (1,))
+    gather(1, 0, first_b)
     site_own, dact_own, dinv = energy(forward(1, 0), *energy_own(0))
     backward(1, 0, dinv, False)
-    before = energy_own(1)
-    wait_in(1)
-    gather(1, 1, first_b, recv_buf[1].T.astype(BF16))
-    site_ghost, dact_ghost, dinv = energy(forward(1, 1), *before)
-    backward(1, 1, dinv, False)
-    send_buf[2] = dot_nt(oh_ghost[atoms:], cot_feat[1])
-    send(2, True)
-    site_out[...] = jnp.where(low_of(site_own), site_own, site_ghost)
-
+    backward(1, 1, dinv_ghost, False)
     cot_own, cot_ghost = dot(rh_c, dact_own), dot(rh_c, dact_ghost)
     cot = rl_col + jnp.where(low_of(cot_own), cot_own, cot_ghost)
     cot = cot + dot_nt(cot_feat[0], oh_own[...]) + dot_nt(cot_feat[1], oh_ghost[:atoms])
-    sums = []
-    for g in range(2):
+
+    def local_backward(g):
         backward(0, g, dot(mix_c[...], split_rows(dup(cot, g))), True)
-        sums.append(edge_grads(g))
+        return edge_grads(g)
+
+    sums_ghost = local_backward(1)
     outward = dot_nt(oh_ghost[atoms:], grad_cat[1])
-    local = dot_nt(grad_cat[0], oh_own[...]) + dot_nt(grad_cat[1], oh_ghost[:atoms])
+
+    wait_in(2)
+    edge_backward(dot(mix_c[...], split_rows(dot(arrived(2), rep[1]))))
+    sums = edge_grads(2)
+    width = counts[2] * atoms
+    outward = outward + dot_nt(oh_edge[atoms:], grad_cat[2, :, :width])
+    rest = outward - outward.astype(BF16).astype(F32)
+    fill(3, jnp.where(lax.broadcasted_iota(jnp.int32, rest.shape, 1) < 16, outward, rest))
+    send(3, True)
+
+    site_out[...] = jnp.where(low_of(site_own), site_own, site_ghost)
+    sums_own = local_backward(0)
+    local = dot_nt(grad_cat[0, :16], oh_own[...]) + dot_nt(grad_cat[1, :16], oh_ghost[:atoms])
+    local = local + dot_nt(grad_cat[2, :16, :width], oh_edge[:atoms])
     mine = jnp.concatenate(
-        [jnp.where(low_of(sums[0][k]), sums[0][k], sums[1][k]) for k in range(3)], axis=0
+        [jnp.where(low_of(sums_own[k]), sums_own[k], sums_ghost[k]) for k in range(3)], axis=0
     )
     local = local[:3] + local[8:11] + mine
-    send_buf[3] = jnp.zeros((ghosts, atoms), F32)
-
-    wait_in(2)
-    back = recv_buf[2].T
-    high = back.astype(BF16).astype(F32)
-    parts = dot(jnp.concatenate([high, back - high], axis=0).astype(BF16), rep[1])
-    dinv = dot(mix_c[...], split_rows(parts[:channels] + parts[channels:]))
-    backward(0, 2, dinv, False)
-    sums = edge_grads(2)
-    width = counts[2] * atoms
-    send_buf[3, :, 0:16] = outward + dot_nt(oh_edge[atoms:], grad_cat[2, :, :width])
-    send(3, True)
-    parts = dot_nt(grad_cat[2, :, :width], oh_edge[:atoms])
-    local = local + parts[:3] + parts[8:11]
     rows = jnp.concatenate(sums + [jnp.zeros((5, atoms), F32)], axis=0)
     rows = jnp.where(lane < few, rows, 0.0)
-
-    def exact(x, chooser):
-        high = x.astype(BF16).astype(F32)
-        mid = (x - high).astype(BF16).astype(F32)
-        out = dot(jnp.concatenate([high, mid, x - high - mid], axis=0).astype(BF16), chooser)
-        return out[:3] + out[8:11] + out[16:19]
-
-    local = local + exact(rows, sel_b[...])
-    wait_in(3)
-    back = recv_buf[3].T
-    force_out[...] = local + exact(back[:8] + back[8:16], sel[...])
+    high = rows.astype(BF16).astype(F32)
+    mid = (rows - high).astype(BF16).astype(F32)
+    parts = jnp.concatenate([high, mid, rows - high - mid], axis=0).astype(BF16)
+    parts = dot(parts, sel_b[...])
+    local = local + (parts[:3] + parts[8:11] + parts[16:19])
     for phase in range(4):
         wait_out(phase)
+    wait_in(3)
+    back = dot(arrived(3)[:32], sel[...])
+    back = back[:16] + back[16:]
+    force_out[...] = local + (back[:3] + back[8:11])
 
 
 def finish(site_in, force_in, site_out, force_out):
@@ -597,7 +704,9 @@
         slots = neighbours.shape[0]
         pairs = slots // 2
         hidden = radial_mid.shape[1]
-        ghosts = plan_slabs(send_list.shape[3])[1]
+        cell_rows = send_list.shape[3]
+        ghosts = plan_slabs(cell_rows)[1]
+        kinds = ((6, 4 * cell_rows), (12, 2 * cell_rows), (8, 2 * cell_rows))
         vmem = pl.BlockSpec(memory_space=pltpu.VMEM)
         operands = (
             species.reshape(1, atoms),
@@ -631,7 +740,7 @@
                 pltpu.VMEM((5, 9, channels, atoms), F32),
                 pltpu.VMEM((2, channels, pairs * atoms), BF16),
                 pltpu.VMEM((3, 9, 8 * pairs, atoms), F32),
-                pltpu.VMEM((3, 16, pairs * atoms), BF16),
+                pltpu.VMEM((3, 32, pairs * atoms), BF16),
                 pltpu.VMEM((ghosts, atoms), BF16),
                 pltpu.VMEM((atoms, atoms), BF16),
                 pltpu.VMEM((2, ghosts, atoms), BF16),
@@ -641,10 +750,12 @@
                 pltpu.VMEM((channels, 9 * channels), BF16),
                 pltpu.VMEM((3 * channels, 3 * channels), BF16),
                 pltpu.VMEM((channels, atoms), F32),
-                pltpu.VMEM((4, ghosts, channels), F32),
-                pltpu.VMEM((4, ghosts, channels), F32),
-                pltpu.SemaphoreType.DMA((4,)),
-                pltpu.SemaphoreType.DMA((4,)),
+                tuple(pltpu.VMEM((4, n, depth, channels), BF16) for n, depth in kinds),
+                tuple(pltpu.VMEM((4, n, depth, channels), BF16) for n, depth in kinds),
+                pltpu.SemaphoreType.DMA((4, len(kinds))),
+                pltpu.SemaphoreType.DMA((4, len(kinds))),
+                pltpu.VMEM((pairs, 2 * channels, atoms), F32),
+                pltpu.VMEM((pairs // 2, 9, channels, atoms), F32),
                 tuple(
                     (pltpu.SMEM if x is send_list else pltpu.VMEM)(x.shape, x.dtype)
                     for x in operands

time: 39.6 us -> 37.7 us (0.952)
  Pallas kernels: 38.9 us -> 36.9 us
    pallas_call x1, Pallas kernels: 38.3 us -> 36.3 us  [body(): pl.pallas_call(functools.partial(kernel, sizes), out_shape=(pltpu.VMEM((1...]
where the time goes in v3:
time: 37.7 us; the launch traced here: 37.5 us
  Pallas kernels  36.9 us (98%)
  between operations  0.64 us (2%)
    pallas_call x1, Pallas kernels, body(): pl.pallas_call(functools.partial(kernel, sizes), out_shape=(pltpu.VMEM((1...  36.3 us

profile of v3, /device:TPU:1, one launch (start us, length us, event | category | flops | bytes accessed | tf_op | source)
XLA Modules:
  0.0 37.5 jit_solution(9384959522351019297)
XLA Ops:
  0.6 36.3 %shard_map.131 = (f32[1,128]{1,0:T(1,128)S(1)}, f32[3,128]{1,0:T(4,128)S(1)}) custom-call(s32[1,128]{1,0:T(1,128)} %bitcast.5, s32[2,2,2,4]{3,2,1,0:T(2,128)} %operands_1_.1, s32[16,128]{1,0:T(8,128)} %operands_2_.1, f32[3,16,128]{2,1,0:T(8,128)} %operands_3_.1, bf16[8,128]{1,0:T(8,128)(2,1)} %operands_4_.1, f32[2,8,64]{2,1,0:T(8,128)} %operands_5_.1, ...), custom_call_target="tpu_custom_call" | custom-call | tf_op jit(solution)/shard_map/pallas_call | solution.py:725
  36.9 0.6 %shard_map.132 = (f32[128]{0:T(128)}, f32[3,128]{1,0:T(4,128)}) custom-call(f32[1,128]{1,0:T(1,128)S(1)} %get-tuple-element.4.site_in, f32[3,128]{1,0:T(4,128)S(1)} %get-tuple-element.5.force_in), custom_call_target="tpu_custom_call" | custom-call | tf_op jit(solution)/shard_map/pallas_call | solution.py:770

commit v4 on v3

--- a/solution.py
+++ b/solution.py
@@ -90,6 +90,7 @@
     sel,
     sel_b,
     rep,
+    rep_t,
     w_in,
     w_mid,
     w_out,
@@ -181,7 +182,7 @@
             ).astype(BF16)
             start += count * depth
 
-    def arrived(phase):
+    def arrived(phase, turned=True):
         parts = []
         for buf in recv_buf:
             block = buf[phase]
@@ -189,7 +190,8 @@
             if depth % 16:
                 block = block.astype(F32).reshape(count * depth, width).astype(BF16)
             parts.append(block.reshape(count * depth, width))
-        return jnp.concatenate(parts, axis=0).T
+        whole = jnp.concatenate(parts, axis=0)
+        return whole.T if turned else whole
 
     lane = lax.broadcasted_iota(jnp.int32, (8, atoms), 1)
     sub = lax.broadcasted_iota(jnp.int32, (8, atoms), 0)
@@ -254,8 +256,8 @@
                 base_b = ghost_row(step, cell_b, atoms, cell_rows) + sub - cell_rows
             row_ids.append(jnp.where(sub < cell_rows, base_a, base_b))
     sel[...] = jnp.concatenate(chosen, axis=0).astype(BF16)
-    rep[0] = jnp.concatenate(rep_one, axis=0).astype(BF16)
-    rep[1] = jnp.concatenate(rep_all, axis=0).astype(BF16)
+    rep[...] = jnp.concatenate(rep_one, axis=0).astype(BF16)
+    rep_t[...] = jnp.concatenate(rep_all, axis=0).T.astype(BF16)
     boundary = []
     for i in range(0, 8, 2):
         ids = jnp.where(sub < cell_rows, cell_ids[cells[i]], cell_ids[cells[i + 1]])
@@ -267,7 +269,7 @@
     start_t = dot(emb_t, kinds)
     start_b = start_t.astype(BF16)
     start_edge = dot_nt(start_b, sel_b[...])
-    fill(0, dot_nt(rep[0], start_edge.astype(BF16)))
+    fill(0, dot_nt(rep[...], start_edge.astype(BF16)))
 
     for t in range(2):
         pad = jnp.zeros((8, hidden), F32)
@@ -398,17 +400,14 @@
         loop(-(-counts[g] // WIDE), chunk)
 
     def gather(t, g, rows_t, ghosts_too=False):
-        for j in range(counts[g] // 2):
-            lanes = slice(j * 2 * atoms, (j + 1) * 2 * atoms)
-            first, second = tiles(t, g) + 2 * j, tiles(t, g) + 2 * j + 1
-            if ghosts_too:
-                out = dot(rows_t, onehots[g][atoms:, lanes])
-                feat[first] = feat[first] + out[:, :atoms]
-                feat[second] = feat[second] + out[:, atoms:]
-            else:
-                out = dot(rows_t, onehots[g][:atoms, lanes])
-                feat[first] = out[:, :atoms]
-                feat[second] = out[:, atoms:]
+        base = tiles(t, g)
+        if ghosts_too:
+            out = dot(rows_t, onehots[g][atoms:])
+        else:
+            out = dot(rows_t, onehots[g][:atoms])
+        for p in range(counts[g]):
+            tile = out[:, p * atoms : (p + 1) * atoms]
+            feat[base + p] = feat[base + p] + tile if ghosts_too else tile
 
     def twin(y):
         return jnp.concatenate([y, y], axis=0)
@@ -502,6 +501,8 @@
         base = tiles(0, 2)
         for p in range(counts[2]):
             ys = [twin(harm[2 * pairs + p, m * 8 : (m + 1) * 8]) for m in range(8)]
+            unit = [y * (1.0 / ROOT3) for y in ys[:3]]
+            over = jnp.broadcast_to(geo[2][3][p : p + 1], (16, atoms))
             for c in range(0, channels, 16):
                 v = 2.0 * feat[base + p, c : c + 16]
                 r = [rad[base + p, l * channels + c : l * channels + c + 16] for l in range(3)]
@@ -510,66 +511,78 @@
                 t1 = ys[0] * a[0] + ys[1] * a[1] + ys[2] * a[2]
                 t2 = ys[3] * a[3] + ys[4] * a[4] + ys[5] * a[5] + ys[6] * a[6] + ys[7] * a[7]
                 p1, p2 = ROOT3 * (v * r[1]), ROOT5 * (v * r[2])
-                out = (
-                    0.5 * v * q[0],
-                    v * q[1] * t1,
-                    v * q[2] * t2,
-                    p1 * a[0],
-                    p1 * a[1],
-                    p1 * a[2],
-                    p2 * (ys[1] * a[3] + ys[2] * a[6] + ys[0] * a[7]),
-                    p2 * (ys[0] * a[3] + ys[2] * a[4] - ys[1] * a[7]),
-                    p2 * (ys[1] * a[4] + ys[0] * a[6] + ROOT3 * (ys[2] * a[5])),
+                along = (0.5 * v * q[0], v * q[1] * t1, v * q[2] * t2)
+                across = (
+                    None,
+                    (p1 * a[0], p1 * a[1], p1 * a[2]),
+                    (
+                        p2 * (ys[1] * a[3] + ys[2] * a[6] + ys[0] * a[7]),
+                        p2 * (ys[0] * a[3] + ys[2] * a[4] - ys[1] * a[7]),
+                        p2 * (ys[1] * a[4] + ys[0] * a[6] + ROOT3 * (ys[2] * a[5])),
+                    ),
                 )
-                for i, x in enumerate(out):
-                    edge_jac[p, i, c : c + 16] = x
+                for l in range(3):
+                    rise, tilt = along[l], across[l]
+                    if tilt is not None:
+                        inward = unit[0] * tilt[0] + unit[1] * tilt[1] + unit[2] * tilt[2]
+                        rise = rise - inward * over
+                    for k in range(3):
+                        x = unit[k] * rise
+                        if tilt is not None:
+                            x = x + tilt[k] * over
+                        edge_jac[p, 3 * l + k, c : c + 16] = x
+
+    def place_rows(g, p, rows):
+        rows = jnp.concatenate(rows + [jnp.zeros((8, atoms), F32)], axis=0)
+        high = rows.astype(BF16).astype(F32)
+        both = jnp.concatenate([high, rows - high], axis=0).astype(BF16)
+        lanes = slice(p * atoms, (p + 1) * atoms)
+        grad_cat[g, :half, lanes] = both
+        grad_cat[g, half:, lanes] = both
 
     def edge_backward(dinv):
+        sums = [0.0, 0.0, 0.0]
         for p in range(counts[2]):
-            total = [jnp.zeros((16, atoms), F32) for _ in range(4)]
+            total = [jnp.zeros((16, atoms), F32) for _ in range(3)]
             for c in range(0, channels, 16):
                 d = [dinv[l * channels + c : l * channels + c + 16] for l in range(3)]
-                x = [edge_jac[p, i, c : c + 16] for i in range(9)]
-                total[0] = total[0] + (x[0] * d[0] + x[1] * d[1] + x[2] * d[2])
                 for k in range(3):
-                    total[1 + k] = total[1 + k] + (x[3 + k] * d[1] + x[6 + k] * d[2])
-            for m in range(4):
-                acc_ref[2, m, p * 8 : (p + 1) * 8] = total[m][:8] + total[m][8:]
+                    x = [edge_jac[p, 3 * l + k, c : c + 16] for l in range(3)]
+                    total[k] = total[k] + (x[0] * d[0] + x[1] * d[1] + x[2] * d[2])
+            rows = [t[:8] + t[8:] for t in total]
+            place_rows(2, p, [-r for r in rows])
+            sums = [a + b for a, b in zip(sums, rows)]
+        return sums
 
     def edge_grads(g):
-        n = counts[g]
         d = []
-        for m in range(4 if g == 2 else 9):
-            d.append(sum(acc_ref[g, m, pl.ds(j, n, stride=8), :] for j in range(8)))
-        nx, ny, nz, over = [v[:n] for v in geo[g]]
-        if g == 2:
-            gx, gy, gz = d[1:]
-        else:
-            gx = ROOT3 * d[1] + ROOT15 * (ny * d[4] + nz * d[7] + nx * d[8])
-            gy = ROOT3 * d[2] + ROOT15 * (nx * d[4] + nz * d[5] - ny * d[8])
-            gz = ROOT3 * d[3] + ROOT15 * (ny * d[5] + nx * d[7]) + (3.0 * ROOT5) * nz * d[6]
+        for m in range(9):
+            d.append(sum(acc_ref[g, m, pl.ds(j, pairs, stride=8), :] for j in range(8)))
+        nx, ny, nz, over = geo[g]
+        gx = ROOT3 * d[1] + ROOT15 * (ny * d[4] + nz * d[7] + nx * d[8])
+        gy = ROOT3 * d[2] + ROOT15 * (nx * d[4] + nz * d[5] - ny * d[8])
+        gz = ROOT3 * d[3] + ROOT15 * (ny * d[5] + nx * d[7]) + (3.0 * ROOT5) * nz * d[6]
         along = d[0] - (nx * gx + ny * gy + nz * gz) * over
         grad = [a * along + b * over for a, b in ((nx, gx), (ny, gy), (nz, gz))]
-        basis[g, 0, 0:64] = jnp.zeros((64, atoms), F32)
-        for k in range(3):
-            basis[g, 0, k * 8 : k * 8 + n] = -grad[k]
-        for p in range(n):
-            row = basis[g, 0, pl.ds(p, 8, stride=8), :]
-            high = row.astype(BF16).astype(F32)
-            both = jnp.concatenate([high, row - high], axis=0).astype(BF16)
-            lanes = slice(p * atoms, (p + 1) * atoms)
-            grad_cat[g, 0:16, lanes] = both
-            grad_cat[g, 16:32, lanes] = both
+        for p in range(pairs):
+            rows = [jnp.where(sub == 0, jnp.broadcast_to(-v[p : p + 1], (8, atoms)), 0.0) for v in grad]
+            place_rows(g, p, rows)
         return [fold(jnp.sum(v, axis=0, keepdims=True), g) for v in grad]
 
-    pl.semaphore_wait(barrier, len(slabs))
-    send(0, False)
+    def components(x):
+        x = x[: half // 2] + x[half // 2 : half]
+        return jnp.concatenate(
+            [jnp.sum(x[8 * k : 8 * k + 8], axis=0, keepdims=True) for k in range(3)], axis=0
+        )
+
     onehot(2)
     radial(2, (0,))
     gather(0, 2, start_b)
+    pl.semaphore_wait(barrier, len(slabs))
+    send(0, False)
     mix_t[...] = weight_rows(mixing[0]).T.astype(BF16)
     onehot(1)
-    radial(1, (0, 1))
+    radial(1, (0,))
     gather(0, 1, start_b)
     onehot(0)
     radial(0, (0,))
@@ -579,7 +592,7 @@
     ghost_t = arrived(0)
     gather(0, 2, ghost_t, True)
     first_edge = start_edge + dot(mix_t[...], split_rows(forward(0, 2)))
-    fill(1, dot_nt(rep[0], first_edge.astype(BF16)))
+    fill(1, dot_nt(rep[...], first_edge.astype(BF16)))
     send(1, False)
     gather(0, 1, ghost_t, True)
     inv_own = forward(0, 0)
@@ -587,6 +600,7 @@
     first_b = (start_t + dot(mix_t[...], split_rows(inv_both))).astype(BF16)
     first_ref[...] = first_b.astype(F32)
     gather(1, 1, first_b)
+    radial(1, (1,))
 
     rl_col = jnp.broadcast_to(read_linear[...], (channels, channels)).T
     rh = read_hidden[...]
@@ -620,8 +634,8 @@
     wait_in(1)
     gather(1, 1, arrived(1), True)
     features = forward(1, 1)
+    site_ghost, dact_ghost, dinv_ghost = energy(features, *before)
     early_cot()
-    site_ghost, dact_ghost, dinv_ghost = energy(features, *before)
     late_cot(dinv_ghost)
     fill(2, dot_nt(oh_ghost[atoms:], cot_feat[1]))
     send(2, True)
@@ -646,22 +660,25 @@
     outward = dot_nt(oh_ghost[atoms:], grad_cat[1])
 
     wait_in(2)
-    edge_backward(dot(mix_c[...], split_rows(dot(arrived(2), rep[1]))))
-    sums = edge_grads(2)
+    back = dot(rep_t[...], arrived(2, False))
+    high = back.astype(BF16).astype(F32)
+    back = jnp.concatenate([high, back - high, high], axis=1).astype(BF16)
+    sums = edge_backward(dot_nt(mix_c[...], back))
     width = counts[2] * atoms
     outward = outward + dot_nt(oh_edge[atoms:], grad_cat[2, :, :width])
     rest = outward - outward.astype(BF16).astype(F32)
-    fill(3, jnp.where(lax.broadcasted_iota(jnp.int32, rest.shape, 1) < 16, outward, rest))
+    fill(3, jnp.where(low_of(rest), outward, rest))
     send(3, True)
 
     site_out[...] = jnp.where(low_of(site_own), site_own, site_ghost)
     sums_own = local_backward(0)
-    local = dot_nt(grad_cat[0, :16], oh_own[...]) + dot_nt(grad_cat[1, :16], oh_ghost[:atoms])
-    local = local + dot_nt(grad_cat[2, :16, :width], oh_edge[:atoms])
+    local = dot_nt(grad_cat[0, :half], oh_own[...]) + dot_nt(grad_cat[1, :half], oh_ghost[:atoms])
+    local = local + dot_nt(grad_cat[2, :half, :width], oh_edge[:atoms])
     mine = jnp.concatenate(
         [jnp.where(low_of(sums_own[k]), sums_own[k], sums_ghost[k]) for k in range(3)], axis=0
     )
-    local = local[:3] + local[8:11] + mine
+    local = components(local) + mine
+    sums = [fold(jnp.sum(v, axis=0, keepdims=True), 2) for v in sums]
     rows = jnp.concatenate(sums + [jnp.zeros((5, atoms), F32)], axis=0)
     rows = jnp.where(lane < few, rows, 0.0)
     high = rows.astype(BF16).astype(F32)
@@ -672,9 +689,8 @@
     for phase in range(4):
         wait_out(phase)
     wait_in(3)
-    back = dot(arrived(3)[:32], sel[...])
-    back = back[:16] + back[16:]
-    force_out[...] = local + (back[:3] + back[8:11])
+    back = dot(arrived(3), sel[...])
+    force_out[...] = local + components(back[:half] + back[half:])
 
 
 def finish(site_in, force_in, site_out, force_out):
@@ -740,10 +756,11 @@
                 pltpu.VMEM((5, 9, channels, atoms), F32),
                 pltpu.VMEM((2, channels, pairs * atoms), BF16),
                 pltpu.VMEM((3, 9, 8 * pairs, atoms), F32),
-                pltpu.VMEM((3, 32, pairs * atoms), BF16),
+                pltpu.VMEM((3, atoms, pairs * atoms), BF16),
                 pltpu.VMEM((ghosts, atoms), BF16),
                 pltpu.VMEM((atoms, atoms), BF16),
-                pltpu.VMEM((2, ghosts, atoms), BF16),
+                pltpu.VMEM((ghosts, atoms), BF16),
+                pltpu.VMEM((atoms, ghosts), BF16),
                 pltpu.VMEM((2 * hidden, 32), BF16),
                 pltpu.VMEM((2, hidden, 3 * hidden), BF16),
                 pltpu.VMEM((2, 3 * channels, 3 * hidden), BF16),

time: 37.7 us -> 37.6 us (level)
  no operation moved by 1% of the time
where the time goes in v4:
time: 37.6 us; the launch traced here: 37.5 us
  Pallas kernels  36.9 us (98%)
  between operations  0.64 us (2%)
    pallas_call x1, Pallas kernels, body(): pl.pallas_call(functools.partial(kernel, sizes), out_shape=(pltpu.VMEM((1...  36.3 us

profile of v4, /device:TPU:1, one launch (start us, length us, event | category | flops | bytes accessed | tf_op | source)
XLA Modules:
  0.0 37.5 jit_solution(9057232363624424978)
XLA Ops:
  0.6 36.3 %shard_map.131 = (f32[1,128]{1,0:T(1,128)S(1)}, f32[3,128]{1,0:T(4,128)S(1)}) custom-call(s32[1,128]{1,0:T(1,128)} %bitcast.5, s32[2,2,2,4]{3,2,1,0:T(2,128)} %operands_1_.1, s32[16,128]{1,0:T(8,128)} %operands_2_.1, f32[3,16,128]{2,1,0:T(8,128)} %operands_3_.1, bf16[8,128]{1,0:T(8,128)(2,1)} %operands_4_.1, f32[2,8,64]{2,1,0:T(8,128)} %operands_5_.1, ...), custom_call_target="tpu_custom_call" | custom-call | tf_op jit(solution)/shard_map/pallas_call | solution.py:741
  36.9 0.6 %shard_map.132 = (f32[128]{0:T(128)}, f32[3,128]{1,0:T(4,128)}) custom-call(f32[1,128]{1,0:T(1,128)S(1)} %get-tuple-element.4.site_in, f32[3,128]{1,0:T(4,128)S(1)} %get-tuple-element.5.force_in), custom_call_target="tpu_custom_call" | custom-call | tf_op jit(solution)/shard_map/pallas_call | solution.py:787
